TPU v7x, 32 devices: a whole 2x2x4 slice. The times are simulated.
32 devices in a mesh: dp: 16 (over z, y, x), tensor: 2 (over core).
Axes of the slice: x: 2, y: 2, z: 4, core: 2. Of those that a mesh axis runs over, the one named last changes fastest.
Arguments:
- hidden: bfloat16 [2048, 5120], P('dp', 'tensor'), may hold values from -6 to 6
- queries: bfloat16 [2048, 8192], P('dp', 'tensor'), may hold values from -21 to 21
- out_grad: bfloat16 [2048, 8192], P('dp', 'tensor'), may hold values from -16 to 16
- w_key: bfloat16 [5120, 1024], P(None, 'tensor'), may hold values from -0.078125 to 0.078125
- w_value: bfloat16 [5120, 1024], P(None, 'tensor'), may hold values from -0.078125 to 0.078125
- prompt_kv: bfloat16 [16, 2, 1024, 1024], P('dp', None, None, 'tensor'), may hold values from -6 to 6
- block_dest: int32 [16], replicated, may hold values from 0 to 15, as said below
- resp_len: int32 [16], replicated, may hold values from 1 to 128, as said below
Outputs:
- grad_query: bfloat16 [2048, 8192], P('dp', 'tensor')
- grad_hidden: bfloat16 [2048, 5120], P('dp', 'tensor')
- grad_prompt_kv: bfloat16 [16, 2, 1024, 1024], P('dp', None, None, 'tensor')
Inputs may be any that keep to these rules, and one draw needn't show every extreme that they name: block_dest[b] // 4 == b // 4; no shard is the destination of more than 3 blocks, and in every draw some shard is the destination of exactly 3. `resp_len`: some block is full in every draw.
All inputs are finite; a program needn't handle non-finite values.
Results may differ from a plain program's by a relative error of at most 0.019.
Values may be sent and summed in bfloat16 or wider, within the bound.
No kernel may reach another device: no remote copies, remote signals or barrier semaphores. Data moves between devices by JAX's collectives and lax.ppermute only.
A program may use at most 128 MiB of HBM per device.

v0:
```python
import math

import jax
import jax.numpy as jnp
from jax import lax
from jax.sharding import PartitionSpec as P

HD = 128
GROUP = 4
CAP = 3


big_negative = -1e30


def from_behind(block, axis, distance):
    devices = range(lax.axis_size(axis))
    route = [(i - distance, i) for i in devices if i - distance in devices]
    return lax.ppermute(block, axis, route)


def block_grads(query_rows, resp_keys, resp_values, upstream_rows, prompt_pair, length):
    row_count = query_rows.shape[0]
    kv_cols = resp_keys.shape[1]
    kv_heads = kv_cols // HD
    group_size = query_rows.shape[1] // kv_cols
    group_cols = group_size * HD
    score_scale = 1.0 / math.sqrt(HD)
    prompt_len = prompt_pair.shape[1]
    all_keys = jnp.concatenate([prompt_pair[0], resp_keys], axis=0)
    all_values = jnp.concatenate([prompt_pair[1], resp_values], axis=0)
    key_count = all_keys.shape[0]
    row_pos = lax.broadcasted_iota(jnp.int32, (row_count, key_count), 0)
    col_pos = lax.broadcasted_iota(jnp.int32, (row_count, key_count), 1) - prompt_len
    visible = (col_pos < 0) | (col_pos <= row_pos) & (col_pos < length)
    live_rows = lax.broadcasted_iota(jnp.int32, (row_count, 1, 1), 0) < length
    query_grads = []
    key_grads = []
    value_grads = []
    for kv_head in range(kv_heads):
        query_head = query_rows[:, kv_head * group_cols : (kv_head + 1) * group_cols].reshape(
            row_count, group_size, HD
        )
        key_head = all_keys[:, kv_head * HD : (kv_head + 1) * HD]
        value_head = all_values[:, kv_head * HD : (kv_head + 1) * HD]
        upstream_head = upstream_rows[:, kv_head * group_cols : (kv_head + 1) * group_cols].reshape(
            row_count, group_size, HD
        )
        upstream_head = jnp.where(live_rows, upstream_head, jnp.zeros((), jnp.bfloat16))
        scores = (
            jnp.einsum("igd,jd->gij", query_head, key_head, preferred_element_type=jnp.float32)
            * score_scale
        )
        scores = jnp.where(visible[None], scores, big_negative)
        row_peak = jnp.max(scores, axis=2, keepdims=True)
        exponent = jnp.exp(scores - row_peak)
        softmax_out = exponent / jnp.sum(exponent, axis=2, keepdims=True)
        weights = softmax_out.astype(jnp.bfloat16)
        attended = jnp.einsum(
            "gij,jd->igd", weights, value_head, preferred_element_type=jnp.float32
        )
        row_dot = jnp.sum(upstream_head.astype(jnp.float32) * attended, axis=2)
        prob_grad = jnp.einsum(
            "igd,jd->gij", upstream_head, value_head, preferred_element_type=jnp.float32
        )
        score_grad = (softmax_out * (prob_grad - row_dot.T[:, :, None])).astype(jnp.bfloat16)
        query_grad = (
            jnp.einsum("gij,jd->igd", score_grad, key_head, preferred_element_type=jnp.float32)
            * score_scale
        )
        query_grads.append(query_grad.astype(jnp.bfloat16).reshape(row_count, group_cols))
        key_grads.append(
            jnp.einsum("gij,igd->jd", score_grad, query_head, preferred_element_type=jnp.float32)
            * score_scale
        )
        value_grads.append(
            jnp.einsum("gij,igd->jd", weights, upstream_head, preferred_element_type=jnp.float32)
        )
    grad_query = jnp.concatenate(query_grads, axis=1)
    key_grad = jnp.concatenate(key_grads, axis=1)
    value_grad = jnp.concatenate(value_grads, axis=1)
    prompt_grad = jnp.stack([key_grad[:prompt_len], value_grad[:prompt_len]]).astype(jnp.bfloat16)
    return (
        grad_query,
        key_grad[prompt_len:].astype(jnp.bfloat16),
        value_grad[prompt_len:].astype(jnp.bfloat16),
        prompt_grad,
    )


def holder_slots(stacked, is_valid, lengths, prompt_pair, query_cols, kv_cols):
    slot_total = stacked.shape[0]
    slot_ids = jnp.arange(slot_total, dtype=jnp.int32)
    slot_order = jnp.argsort(jnp.where(is_valid, slot_ids, slot_ids + slot_total))[:CAP]
    chosen_valid = is_valid[slot_order]
    prompt_sum = jnp.zeros(prompt_pair.shape, jnp.float32)
    results = []
    for slot_number in range(CAP):
        block_data = stacked[slot_order[slot_number]]
        grad_query, grad_key, grad_value, prompt_grad = block_grads(
            block_data[:, :query_cols],
            block_data[:, query_cols : query_cols + kv_cols],
            block_data[:, query_cols + kv_cols : query_cols + 2 * kv_cols],
            block_data[:, query_cols + 2 * kv_cols :],
            prompt_pair,
            lengths[slot_order[slot_number]],
        )
        prompt_sum = prompt_sum + jnp.where(
            chosen_valid[slot_number], prompt_grad.astype(jnp.float32), 0.0
        )
        results.append(jnp.concatenate([grad_query, grad_key, grad_value], axis=1))
    outgoing_list = []
    for position in range(slot_total):
        outgoing = jnp.zeros_like(results[0])
        for slot_number in range(CAP):
            taken = (slot_order[slot_number] == position) & chosen_valid[slot_number]
            outgoing = jnp.where(taken, results[slot_number], outgoing)
        outgoing_list.append(outgoing)
    return (prompt_sum.astype(jnp.bfloat16)[None], outgoing_list)


def local(hidden, queries, out_grad, w_key, w_value, prompt_kv, block_dest, resp_len):
    own_index = lax.axis_index("dp")
    nblocks = block_dest.shape[0]
    full_hidden = lax.all_gather(hidden, "tensor", axis=1, tiled=True)
    resp_keys = jnp.dot(full_hidden, w_key, preferred_element_type=jnp.float32).astype(jnp.bfloat16)
    resp_values = jnp.dot(full_hidden, w_value, preferred_element_type=jnp.float32).astype(
        jnp.bfloat16
    )
    own_offset = block_dest[own_index] - own_index
    offsets = list(range(1 - GROUP, GROUP))
    query_cols = queries.shape[1]
    kv_cols = resp_keys.shape[1]
    packed = jnp.concatenate([queries, resp_keys, resp_values, out_grad], axis=1)
    arrived = []
    for offset in offsets:
        if offset == 0:
            arrived.append(packed)
        else:
            arrived.append(from_behind(packed, "dp", offset))
    stacked = jnp.stack(arrived)
    sources = own_index - jnp.asarray(offsets, jnp.int32)
    inside = (sources >= 0) & (sources < nblocks)
    safe_sources = jnp.clip(sources, 0, nblocks - 1)
    is_valid = inside & (block_dest[safe_sources] == own_index)
    lengths = resp_len[safe_sources]
    grad_prompt, outgoing_list = holder_slots(
        stacked, is_valid, lengths, prompt_kv[0], query_cols, kv_cols
    )
    own_result = jnp.zeros_like(outgoing_list[0])
    for position, offset in enumerate(offsets):
        if offset == 0:
            returned = outgoing_list[position]
        else:
            returned = from_behind(outgoing_list[position], "dp", -offset)
        own_result = jnp.where(own_offset == offset, returned, own_result)
    grad_query = own_result[:, :query_cols]
    grad_key = own_result[:, query_cols : query_cols + kv_cols]
    grad_value = own_result[:, query_cols + kv_cols :]
    partial_value = jnp.einsum("ic,dc->id", grad_key, w_key, preferred_element_type=jnp.float32)
    partial_value = partial_value + jnp.einsum(
        "ic,dc->id", grad_value, w_value, preferred_element_type=jnp.float32
    )
    summed = lax.psum(partial_value.astype(jnp.bfloat16), "tensor").astype(jnp.float32)
    share_cols = hidden.shape[1]
    grad_hidden = lax.dynamic_slice_in_dim(
        summed, lax.axis_index("tensor") * share_cols, share_cols, 1
    )
    return (grad_query, grad_hidden.astype(jnp.bfloat16), grad_prompt)


def solution(mesh):
    return jax.shard_map(
        local,
        mesh=mesh,
        in_specs=(
            P("dp", "tensor"),
            P("dp", "tensor"),
            P("dp", "tensor"),
            P(None, "tensor"),
            P(None, "tensor"),
            P("dp", None, None, "tensor"),
            P(),
            P(),
        ),
        out_specs=(P("dp", "tensor"), P("dp", "tensor"), P("dp", None, None, "tensor")),
        check_vma=False,
    )
```

profile of v0, /device:TPU:0, one launch (start us, length us, event | category | flops | bytes accessed | tf_op | source)
XLA Modules:
  0.0 752.4 jit_solution(10517214902565838024)
XLA Ops:
  8.0 13.7 %all-gather.2.cloned.1.call-done = bf16[128,5120]{1,0:T(8,128)(2,1)} async-done(((bf16[128,2560]{1,0:T(8,128)(2,1)}), bf16[128,5120]{1,0:T(8,128)(2,1)}) %all-gather.2.cloned.1.call-update) | async-done | bytes 1310736 | tf_op jit(solution)/shard_map/all_gather | solution.py:125
  72.6 4.7 collective-permute-start.3
  77.3 4.6 collective-permute-start.4
  82.0 4.8 collective-permute-done
  92.9 43.7 %collective-permute-done.1 = bf16[128,9216]{1,0:T(8,128)(2,1)S(1)} collective-permute-done((bf16[128,9216]{1,0:T(8,128)(2,1)}, bf16[128,9216]{1,0:T(8,128)(2,1)S(1)}, u32[]{:S(2)}, u32[]{:S(2)}) %collective-permute-start.1) | collective-permute-done | bytes 2359328 | tf_op jit(solution)/shard_map/ppermute | solution.py:19
  138.4 99.7 %collective-permute-done.4 = bf16[128,9216]{1,0:T(8,128)(2,1)S(1)} collective-permute-done((bf16[128,9216]{1,0:T(8,128)(2,1)}, bf16[128,9216]{1,0:T(8,128)(2,1)S(1)}, u32[]{:S(2)}, u32[]{:S(2)}) %collective-permute-start.4) | collective-permute-done | bytes 2359328 | tf_op jit(solution)/shard_map/ppermute | solution.py:19
  244.1 4.8 exponential_reduce_fusion.8
  257.6 4.8 exponential_reduce_fusion.9
  272.5 4.9 exponential_reduce_fusion.10
  286.2 4.8 exponential_reduce_fusion.11
  312.5 4.8 exponential_reduce_fusion.4
  326.9 4.8 exponential_reduce_fusion.5
  343.2 5.0 exponential_reduce_fusion.6
  359.7 4.8 exponential_reduce_fusion.7
  384.4 5.0 exponential_reduce_fusion
  399.1 4.8 exponential_reduce_fusion.1
  415.3 4.8 exponential_reduce_fusion.2
  432.1 4.8 exponential_reduce_fusion.3
  504.3 53.3 %collective-permute-start.9 = (bf16[128,5120]{1,0:T(8,128)(2,1)}, bf16[128,5120]{1,0:T(8,128)(2,1)}, u32[]{:S(2)}, u32[]{:S(2)}) collective-permute-start(bf16[128,5120]{1,0:T(8,128)(2,1)} %get-tuple-element.18), channel_id=1, source_target_pairs={{0,2},{2,4},{4,6},{6,8},{8,10},{10,12},{12,14},{14,16},{16,18},{18... | collective-permute-start | bytes 3932168 | tf_op jit(solution)/shard_map/ppermute | solution.py:19
  557.6 27.9 %collective-permute-start.10 = (bf16[128,5120]{1,0:T(8,128)(2,1)}, bf16[128,5120]{1,0:T(8,128)(2,1)}, u32[]{:S(2)}, u32[]{:S(2)}) collective-permute-start(bf16[128,5120]{1,0:T(8,128)(2,1)} %get-tuple-element.17), channel_id=1, source_target_pairs={{0,4},{2,6},{4,8},{6,10},{8,12},{10,14},{12,16},{14,18},{16,20},{1... | collective-permute-start | bytes 3932168 | tf_op jit(solution)/shard_map/ppermute | solution.py:19
  585.5 17.3 %collective-permute-done.6 = bf16[128,5120]{1,0:T(8,128)(2,1)} collective-permute-done((bf16[128,5120]{1,0:T(8,128)(2,1)S(1)}, bf16[128,5120]{1,0:T(8,128)(2,1)}, u32[]{:S(2)}, u32[]{:S(2)}) %collective-permute-start.6) | collective-permute-done | bytes 1310752 | tf_op jit(solution)/shard_map/ppermute | solution.py:19
  612.1 50.8 %collective-permute-done.10 = bf16[128,5120]{1,0:T(8,128)(2,1)} collective-permute-done((bf16[128,5120]{1,0:T(8,128)(2,1)}, bf16[128,5120]{1,0:T(8,128)(2,1)}, u32[]{:S(2)}, u32[]{:S(2)}) %collective-permute-start.10) | collective-permute-done | bytes 1310752 | tf_op jit(solution)/shard_map/ppermute | solution.py:19
  666.8 5.4 fusion.12
  682.7 60.8 %all-reduce.2.cloned.1.call-done = bf16[128,5120]{1,0:T(8,128)(2,1)} async-done(((bf16[128,5120]{1,0:T(8,128)(2,1)}), bf16[128,5120]{1,0:T(8,128)(2,1)}) %all-reduce.2.cloned.1.call-update) | async-done | bytes 1310736 | tf_op jit(solution)/shard_map/psum | solution.py:164
  (464 shorter events, 260.6 us)
Async XLA Ops:
  7.2 40.0 %copy-start = (s32[16]{0:T(128)S(1)}, s32[16]{0:T(128)}, u32[]{:S(2)}) copy-start(s32[16]{0:T(128)} %param.16) | copy-start | bytes 196
  7.2 14.5 %all-gather.2.cloned.1.call-start = ((), (), s32[]{:S(2)}) async-start(), calls=%async_computation | async-start | bytes 1966080 | tf_op jit(solution)/shard_map/all_gather | solution.py:125
  7.9 735.5 %all-reduce.2.cloned.1.call-start = ((), (), s32[]{:S(2)}) async-start(), calls=%async_computation.1 | async-start | bytes 2621440 | tf_op jit(solution)/shard_map/psum | solution.py:164
  29.6 57.2 %collective-permute-start = (bf16[128,9216]{1,0:T(8,128)(2,1)}, bf16[128,9216]{1,0:T(8,128)(2,1)}, u32[]{:S(2)}, u32[]{:S(2)}) collective-permute-start(bf16[128,9216]{1,0:T(8,128)(2,1)} %pad_maximum_fusion), channel_id=1, source_target_pairs={{6,0},{8,2},{10,4},{12,6},{14,8},{16,10},{18,12},{20,14},{22,16},{... | collective-permute-start | bytes 7077896 | tf_op jit(solution)/shard_map/ppermute | solution.py:19
  68.4 68.2 %collective-permute-start.1 = (bf16[128,9216]{1,0:T(8,128)(2,1)}, bf16[128,9216]{1,0:T(8,128)(2,1)S(1)}, u32[]{:S(2)}, u32[]{:S(2)}) collective-permute-start(bf16[128,9216]{1,0:T(8,128)(2,1)} %pad_maximum_fusion), channel_id=1, source_target_pairs={{4,0},{6,2},{8,4},{10,6},{12,8},{14,10},{16,12},{18,14},{20,16},{2... | collective-permute-start | bytes 7077896 | tf_op jit(solution)/shard_map/ppermute | solution.py:19
  71.3 66.5 %collective-permute-start.2 = (bf16[128,9216]{1,0:T(8,128)(2,1)}, bf16[128,9216]{1,0:T(8,128)(2,1)S(1)}, u32[]{:S(2)}, u32[]{:S(2)}) collective-permute-start(bf16[128,9216]{1,0:T(8,128)(2,1)} %pad_maximum_fusion), channel_id=1, source_target_pairs={{2,0},{4,2},{6,4},{8,6},{10,8},{12,10},{14,12},{16,14},{18,16},{20... | collective-permute-start | bytes 7077896 | tf_op jit(solution)/shard_map/ppermute | solution.py:19
  72.6 65.6 %collective-permute-start.3 = (bf16[128,9216]{1,0:T(8,128)(2,1)}, bf16[128,9216]{1,0:T(8,128)(2,1)S(1)}, u32[]{:S(2)}, u32[]{:S(2)}) collective-permute-start(bf16[128,9216]{1,0:T(8,128)(2,1)} %pad_maximum_fusion), channel_id=1, source_target_pairs={{0,2},{2,4},{4,6},{6,8},{8,10},{10,12},{12,14},{14,16},{16,18},{18... | collective-permute-start | bytes 7077896 | tf_op jit(solution)/shard_map/ppermute | solution.py:19
  77.3 160.7 %collective-permute-start.4 = (bf16[128,9216]{1,0:T(8,128)(2,1)}, bf16[128,9216]{1,0:T(8,128)(2,1)S(1)}, u32[]{:S(2)}, u32[]{:S(2)}) collective-permute-start(bf16[128,9216]{1,0:T(8,128)(2,1)} %pad_maximum_fusion), channel_id=1, source_target_pairs={{0,4},{2,6},{4,8},{6,10},{8,12},{10,14},{12,16},{14,18},{16,20},{1... | collective-permute-start | bytes 7077896 | tf_op jit(solution)/shard_map/ppermute | solution.py:19
  86.8 151.4 %collective-permute-start.5 = (bf16[128,9216]{1,0:T(8,128)(2,1)}, bf16[128,9216]{1,0:T(8,128)(2,1)S(1)}, u32[]{:S(2)}, u32[]{:S(2)}) collective-permute-start(bf16[128,9216]{1,0:T(8,128)(2,1)} %pad_maximum_fusion), channel_id=1, source_target_pairs={{0,6},{2,8},{4,10},{6,12},{8,14},{10,16},{12,18},{14,20},{16,22},{... | collective-permute-start | bytes 7077896 | tf_op jit(solution)/shard_map/ppermute | solution.py:19
  461.0 9.7 %copy-start.52 = (bf16[1152,128]{0,1:T(8,128)(2,1)S(1)}, bf16[1152,128]{0,1:T(8,128)(2,1)}, u32[]{:S(2)}) copy-start(bf16[1152,128]{0,1:T(8,128)(2,1)} %fusion.65) | copy-start | bytes 884740
  461.0 9.6 %copy-start.54 = (bf16[1152,128]{0,1:T(8,128)(2,1)S(1)}, bf16[1152,128]{0,1:T(8,128)(2,1)}, u32[]{:S(2)}) copy-start(bf16[1152,128]{0,1:T(8,128)(2,1)} %fusion.66) | copy-start | bytes 884740
  471.5 11.2 %copy-start.63 = (bf16[1152,128]{0,1:T(8,128)(2,1)S(1)}, bf16[1152,128]{0,1:T(8,128)(2,1)}, u32[]{:S(2)}) copy-start(bf16[1152,128]{0,1:T(8,128)(2,1)} %fusion.61) | copy-start | bytes 884740
  471.5 11.2 %copy-start.65 = (bf16[1152,128]{0,1:T(8,128)(2,1)S(1)}, bf16[1152,128]{0,1:T(8,128)(2,1)}, u32[]{:S(2)}) copy-start(bf16[1152,128]{0,1:T(8,128)(2,1)} %fusion.62) | copy-start | bytes 884740
  471.5 11.2 %copy-start.67 = (bf16[1152,128]{0,1:T(8,128)(2,1)S(1)}, bf16[1152,128]{0,1:T(8,128)(2,1)}, u32[]{:S(2)}) copy-start(bf16[1152,128]{0,1:T(8,128)(2,1)} %fusion.63) | copy-start | bytes 884740
  497.2 111.9 %copy-start.3 = (s32[16]{0:T(128)S(1)}, s32[16]{0:T(128)}, u32[]{:S(2)}) copy-start(s32[16]{0:T(128)} %param.15) | copy-start | bytes 196
  497.2 105.6 %collective-permute-start.6 = (bf16[128,5120]{1,0:T(8,128)(2,1)S(1)}, bf16[128,5120]{1,0:T(8,128)(2,1)}, u32[]{:S(2)}, u32[]{:S(2)}) collective-permute-start(bf16[128,5120]{1,0:T(8,128)(2,1)S(1)} %select_select_fusion.6), channel_id=1, source_target_pairs={{6,0},{8,2},{10,4},{12,6},{14,8},{16,10},{18,12},{20,14},{22,16},{... | collective-permute-start | bytes 3932168 | tf_op jit(solution)/shard_map/ppermute | solution.py:19
  498.6 166.4 %slice-start = ((s8[5242880]{0:T(1024)(128)(4,1)}), s8[1048576]{0:T(1024)(128)(4,1)S(1)}, s32[]{:S(2)}) async-start(s8[5242880]{0:T(1024)(128)(4,1)} %bitcast.664), calls=%async_computation.2 | async-start | bytes 2097152
  501.5 110.6 %collective-permute-start.7 = (bf16[128,5120]{1,0:T(8,128)(2,1)}, bf16[128,5120]{1,0:T(8,128)(2,1)}, u32[]{:S(2)}, u32[]{:S(2)}) collective-permute-start(bf16[128,5120]{1,0:T(8,128)(2,1)} %get-tuple-element.20), channel_id=1, source_target_pairs={{4,0},{6,2},{8,4},{10,6},{12,8},{14,10},{16,12},{18,14},{20,16},{2... | collective-permute-start | bytes 3932168 | tf_op jit(solution)/shard_map/ppermute | solution.py:19
  502.8 109.3 %collective-permute-start.8 = (bf16[128,5120]{1,0:T(8,128)(2,1)}, bf16[128,5120]{1,0:T(8,128)(2,1)}, u32[]{:S(2)}, u32[]{:S(2)}) collective-permute-start(bf16[128,5120]{1,0:T(8,128)(2,1)} %get-tuple-element.19), channel_id=1, source_target_pairs={{2,0},{4,2},{6,4},{8,6},{10,8},{12,10},{14,12},{16,14},{18,16},{20... | collective-permute-start | bytes 3932168 | tf_op jit(solution)/shard_map/ppermute | solution.py:19
  504.3 107.9 %collective-permute-start.9 = (bf16[128,5120]{1,0:T(8,128)(2,1)}, bf16[128,5120]{1,0:T(8,128)(2,1)}, u32[]{:S(2)}, u32[]{:S(2)}) collective-permute-start(bf16[128,5120]{1,0:T(8,128)(2,1)} %get-tuple-element.18), channel_id=1, source_target_pairs={{0,2},{2,4},{4,6},{6,8},{8,10},{10,12},{12,14},{14,16},{16,18},{18... | collective-permute-start | bytes 3932168 | tf_op jit(solution)/shard_map/ppermute | solution.py:19
  557.6 105.4 %collective-permute-start.10 = (bf16[128,5120]{1,0:T(8,128)(2,1)}, bf16[128,5120]{1,0:T(8,128)(2,1)}, u32[]{:S(2)}, u32[]{:S(2)}) collective-permute-start(bf16[128,5120]{1,0:T(8,128)(2,1)} %get-tuple-element.17), channel_id=1, source_target_pairs={{0,4},{2,6},{4,8},{6,10},{8,12},{10,14},{12,16},{14,18},{16,20},{1... | collective-permute-start | bytes 3932168 | tf_op jit(solution)/shard_map/ppermute | solution.py:19
  602.8 60.2 %collective-permute-start.11 = (bf16[128,5120]{1,0:T(8,128)(2,1)}, bf16[128,5120]{1,0:T(8,128)(2,1)}, u32[]{:S(2)}, u32[]{:S(2)}) collective-permute-start(bf16[128,5120]{1,0:T(8,128)(2,1)} %get-tuple-element.16), channel_id=1, source_target_pairs={{0,6},{2,8},{4,10},{6,12},{8,14},{10,16},{12,18},{14,20},{16,22},{... | collective-permute-start | bytes 3932168 | tf_op jit(solution)/shard_map/ppermute | solution.py:19
  612.1 52.9 %slice-start.1 = ((s8[5242880]{0:T(1024)(128)(4,1)}), s8[4194304]{0:T(1024)(128)(4,1)S(1)}, s32[]{:S(2)}) async-start(s8[5242880]{0:T(1024)(128)(4,1)} %bitcast.664), calls=%async_computation.3 | async-start | bytes 8388608
  679.0 66.4 %copy-start.1 = (s32[16]{0:T(128)S(1)}, s32[16]{0:T(128)}, u32[]{:S(2)}) copy-start(s32[16]{0:T(128)} %param.16) | copy-start | bytes 196
  (116 other events, 346.8 us)
Sparse Core Ops, SparseCore 0:
  9.6 12.1 all-gather.1
  672.4 70.9 all-reduce.1
where the time goes:
time: 759 us; the launch traced here: 752 us
  waiting for transfers between devices  293 us (39%)
  matrix products  143 us (19%)
  starting transfers between devices  107 us (14%)
  local copies, waits for them, and re-layouts  98.7 us (13%)
  other arithmetic  64 us (8%)
  between operations  46.5 us (6%)
    ppermute x12, waiting for transfers between devices, from_behind(): return lax.ppermute(block, axis, route)  217 us
    ppermute x12, starting transfers between devices, from_behind(): return lax.ppermute(block, axis, route)  107 us
    psum x1, waiting for transfers between devices, local(): lax.psum(partial_value.astype(jnp.bfloat16), 'tensor').astype(jnp.float32)  60.8 us
    sub x12, matrix products, block_grads(): exponent = jnp.exp(scores - row_peak)  58.5 us
    convert_element_type x12, other arithmetic, block_grads(): weights = softmax_out.astype(jnp.bfloat16)  37.3 us
    unnamed x273, local copies, waits for them, and re-layouts  22.5 us
    reshape x12, local copies, waits for them, and re-layouts, block_grads(): query_grad.astype(jnp.bfloat16).reshape(row_count, group_cols)  20.6 us
    dot_general x12, matrix products, block_grads(): jnp.einsum('gij,igd->jd', weights, upstream_head, preferred_element_type=...  19 us
  transfers between devices with their start and end apart: 14, of which 8 were waited for; matrix products, arithmetic and copies ran while one was open for 4% of the time, Pallas kernels for 0%

commit v1 on v0

v1 whole, which is shorter than its diff:
```python
import functools
import math

import jax
import jax.numpy as jnp
from jax import lax
from jax.experimental import pallas as pl
from jax.experimental.pallas import tpu as pltpu
from jax.sharding import PartitionSpec as P

HD = 128
GROUP = 4
HEADS_AT_ONCE = 2
X_BIT = 1
Y_BIT = 2

big_negative = -1e30


def swap_with(block, axis, bit):
    return lax.ppermute(block, axis, [(i, i ^ bit) for i in range(lax.axis_size(axis))])


def attention_grads_kernel(
    meta_ref,
    queries,
    upstreams,
    resp_kv,
    own_keys,
    own_values,
    x_keys,
    y_keys,
    x_values,
    y_values,
    *refs,
    first,
    heads,
    kv_heads,
    prompt_len,
    group_size,
    aliased,
):
    refs = refs[aliased:]
    outputs, refs = refs[:5], refs[5:]
    query, upstream, keys, values, keys_t, value_grad, key_grad = refs[:7]
    results, (load_sems, store_sems) = refs[7:12], refs[12:]
    mode = meta_ref[0]
    length = meta_ref[1]
    rows = resp_kv.shape[0]
    score_scale = 1.0 / math.sqrt(HD)
    prompt_part = slice(0, prompt_len)
    resp_part = slice(prompt_len, prompt_len + rows)
    group_cols = group_size * HD

    def columns(ref, index, width):
        return ref.at[:, pl.ds(index * width, width)]

    def loads(h):
        key_rows = keys.at[h, pl.ds(0, prompt_len)]
        value_rows = values.at[h, pl.ds(0, prompt_len)]
        key_sources = [
            (mode == 0, own_keys),
            (mode == X_BIT, x_keys),
            (mode >= Y_BIT, y_keys),
        ]
        value_sources = [
            (mode == 0, own_values),
            (mode == Y_BIT, y_values),
            ((mode == X_BIT) | (mode == X_BIT + Y_BIT), x_values),
        ]
        resp_keys = columns(resp_kv, first + h, HD)
        resp_values = columns(resp_kv, kv_heads + first + h, HD)
        return [
            [(flag, columns(ref, h, HD), key_rows) for flag, ref in key_sources],
            [(None, resp_keys, keys.at[h, pl.ds(prompt_len, rows)])],
            [(None, columns(queries, first + h, group_cols), query.at[h])],
            [(flag, columns(ref, h, HD), value_rows) for flag, ref in value_sources],
            [(None, resp_values, values.at[h, pl.ds(prompt_len, rows)])],
            [(None, columns(upstreams, first + h, group_cols), upstream.at[h])],
        ]

    for h in range(heads):
        for slot, choices in enumerate(loads(h)):
            for flag, source, target in choices:
                copy = pltpu.make_async_copy(source, target, load_sems.at[h, slot])
                if flag is None:
                    copy.start()
                else:
                    pl.when(flag)(copy.start)

    key_pos = lax.broadcasted_iota(jnp.int32, (rows, rows), 0)
    row_pos = lax.broadcasted_iota(jnp.int32, (rows, rows), 1)
    visible = (key_pos <= row_pos) & (key_pos < length)
    visible = jnp.concatenate([visible.astype(jnp.int32)] * HEADS_AT_ONCE, axis=1) > 0
    live = lax.broadcasted_iota(jnp.int32, (rows, HD), 0) < length
    live = jnp.concatenate([live.astype(jnp.int32)] * HEADS_AT_ONCE, axis=0) > 0
    nt = (((1,), (1,)), ((), ()))
    tiles = group_size // HEADS_AT_ONCE

    def tile_inputs(h, index):
        if index == 0:
            for slot, choices in enumerate(loads(h)):
                _, source, target = choices[0]
                pltpu.make_async_copy(source, target, load_sems.at[h, slot]).wait()
            keys_t[h] = keys[h].T
        parts = range(index * HEADS_AT_ONCE, (index + 1) * HEADS_AT_ONCE)
        parts = [slice(k * HD, (k + 1) * HD) for k in parts]
        tile_query = jnp.concatenate([query[h, :, part] for part in parts], axis=0)
        tile_upstream = jnp.concatenate([upstream[h, :, part] for part in parts], axis=0)
        tile_upstream = jnp.where(live, tile_upstream, jnp.zeros((), jnp.bfloat16))
        scores = lax.dot_general(keys[h], tile_query, nt, preferred_element_type=jnp.float32)
        prob_grad = lax.dot_general(
            values[h], tile_upstream, nt, preferred_element_type=jnp.float32
        )
        return parts, tile_query, tile_upstream, scores, prob_grad

    def store(h, slot, target):
        copy = pltpu.make_async_copy(results[slot].at[h], target, store_sems.at[h, slot])
        copy.start()
        return copy

    stores = []
    steps = [(h, index) for h in range(heads) for index in range(tiles)]
    following = tile_inputs(*steps[0])
    for step, (h, index) in enumerate(steps):
        parts, tile_query, tile_upstream, scores, prob_grad = following
        if step + 1 < len(steps):
            following = tile_inputs(*steps[step + 1])
        resp_scores = jnp.where(visible, scores[prompt_len:], big_negative)
        scores = jnp.concatenate([scores[:prompt_len], resp_scores], axis=0)
        peak = jnp.max(scores, axis=0, keepdims=True)
        exponent = jnp.exp2((scores - peak) * (score_scale * math.log2(math.e)))
        probs = exponent * (1.0 / jnp.sum(exponent, axis=0, keepdims=True))
        weights = probs.astype(jnp.bfloat16)
        row_dot = jnp.sum(weights.astype(jnp.float32) * prob_grad, axis=0, keepdims=True)
        score_grad = (probs * (prob_grad - row_dot)).astype(jnp.bfloat16)
        value_term = jnp.dot(weights, tile_upstream, preferred_element_type=jnp.float32)
        key_term = jnp.dot(score_grad, tile_query, preferred_element_type=jnp.float32)
        query_grad_t = jnp.dot(keys_t[h], score_grad, preferred_element_type=jnp.float32)
        query_grad = (query_grad_t * score_scale).T.astype(jnp.bfloat16)
        for k, part in enumerate(parts):
            results[0][h, :, part] = query_grad[k * rows : (k + 1) * rows]
        if index > 0:
            value_term = value_grad[...] + value_term
            key_term = key_grad[...] + key_term
        if index + 1 < tiles:
            value_grad[...] = value_term
            key_grad[...] = key_term
            continue
        value_term = value_term.astype(jnp.bfloat16)
        results[2][h] = value_term[resp_part]
        results[4][h] = value_term[prompt_part]
        key_term = (key_term * score_scale).astype(jnp.bfloat16)
        results[1][h] = key_term[resp_part]
        results[3][h] = key_term[prompt_part]
        stores += [
            store(h, 0, columns(outputs[0], first + h, group_cols)),
            store(h, 1, columns(outputs[1], first + h, HD)),
            store(h, 2, columns(outputs[2], first + h, HD)),
            store(h, 3, columns(outputs[3], h, HD)),
            store(h, 4, columns(outputs[4], h, HD)),
        ]
    for copy in stores:
        copy.wait()


def chunk_grads(first, heads, meta, queries, out_grad, resp_kv, sources, prompt_len, earlier):
    rows, query_cols = queries.shape
    kv_cols = resp_kv.shape[1] // 2
    group_size = query_cols // kv_cols
    group_cols = group_size * HD
    key_count = prompt_len + rows
    bf16 = jnp.bfloat16
    part = jax.ShapeDtypeStruct((prompt_len, heads * HD), bf16)
    matmul_flops = 2 * heads * group_size * rows * key_count * HD
    anywhere = pl.BlockSpec(memory_space=pl.ANY)
    return pl.pallas_call(
        functools.partial(
            attention_grads_kernel,
            first=first,
            heads=heads,
            kv_heads=kv_cols // HD,
            prompt_len=prompt_len,
            group_size=group_size,
            aliased=len(earlier),
        ),
        in_specs=[pl.BlockSpec(memory_space=pltpu.SMEM)] + [anywhere] * (9 + len(earlier)),
        out_specs=[anywhere] * 5,
        scratch_shapes=[
            pltpu.VMEM((heads, rows, group_cols), bf16),
            pltpu.VMEM((heads, rows, group_cols), bf16),
            pltpu.VMEM((heads, key_count, HD), bf16),
            pltpu.VMEM((heads, key_count, HD), bf16),
            pltpu.VMEM((heads, HD, key_count), bf16),
            pltpu.VMEM((key_count, HD), jnp.float32),
            pltpu.VMEM((key_count, HD), jnp.float32),
            pltpu.VMEM((heads, rows, group_cols), bf16),
            pltpu.VMEM((heads, rows, HD), bf16),
            pltpu.VMEM((heads, rows, HD), bf16),
            pltpu.VMEM((heads, prompt_len, HD), bf16),
            pltpu.VMEM((heads, prompt_len, HD), bf16),
            pltpu.SemaphoreType.DMA((heads, 6)),
            pltpu.SemaphoreType.DMA((heads, 5)),
        ],
        out_shape=[
            jax.ShapeDtypeStruct((rows, query_cols), bf16),
            jax.ShapeDtypeStruct((rows, kv_cols), bf16),
            jax.ShapeDtypeStruct((rows, kv_cols), bf16),
            part,
            part,
        ],
        input_output_aliases={10 + k: k for k in range(len(earlier))},
        compiler_params=pltpu.CompilerParams(vmem_limit_bytes=32 * 1024 * 1024),
        cost_estimate=pl.CostEstimate(
            flops=10 * matmul_flops,
            bytes_accessed=8 * heads * prompt_len * HD * 2,
            transcendentals=heads * group_size * rows * key_count,
        ),
        name="attention_grads",
    )(meta, queries, out_grad, resp_kv, *sources, *earlier)


def flags_kernel(flags_ref, x_ref, y_ref, held_ref):
    row = lax.broadcasted_iota(jnp.int32, held_ref.shape, 0)
    held = jnp.zeros(held_ref.shape, jnp.int32)
    for k in range(flags_ref.shape[0]):
        held = jnp.where(row == k, flags_ref[k], held)
    held_ref[...] = held


def flags_after(flags, from_x, from_y):
    held = pl.pallas_call(
        flags_kernel,
        in_specs=[pl.BlockSpec(memory_space=pltpu.SMEM)]
        + [pl.BlockSpec(memory_space=pl.ANY)] * 2,
        out_shape=jax.ShapeDtypeStruct((8, HD), jnp.int32),
        cost_estimate=pl.CostEstimate(flops=2 * 10**10, bytes_accessed=0, transcendentals=0),
        name="flags_after",
    )(jnp.stack(flags).astype(jnp.int32), from_x, from_y)
    return [held[k, 0] != 0 for k in range(len(flags))]


def pick(flag, one, other):
    return jnp.where(flag, one, other)


def chunk_heads(kv_heads):
    if kv_heads == 1:
        return [1]
    return [kv_heads // 2, kv_heads - kv_heads // 2]


def masked_sum(first_flag, first, second_flag, second):
    zero = jnp.zeros((), jnp.float32)
    return jnp.where(first_flag, first.astype(jnp.float32), zero) + jnp.where(
        second_flag, second.astype(jnp.float32), zero
    )


def whole_features(hidden):
    if lax.axis_size("tensor") != 2:
        return lax.all_gather(hidden, "tensor", axis=1, tiled=True)
    other = swap_with(hidden, "tensor", 1)
    is_first = lax.axis_index("tensor") == 0
    return jnp.concatenate(
        [pick(is_first, hidden, other), pick(is_first, other, hidden)], axis=1
    )


def summed_share(partial_sum, share_cols):
    if lax.axis_size("tensor") != 2:
        return lax.psum_scatter(
            partial_sum.astype(jnp.bfloat16), "tensor", scatter_dimension=1, tiled=True
        )
    is_first = lax.axis_index("tensor") == 0
    low, high = partial_sum[:, :share_cols], partial_sum[:, share_cols:]
    sent = pick(is_first, high, low).astype(jnp.bfloat16)
    received = swap_with(sent, "tensor", 1).astype(jnp.float32)
    return (pick(is_first, low, high) + received).astype(jnp.bfloat16)


def local(hidden, queries, out_grad, w_key, w_value, prompt_kv, block_dest, resp_len):
    own = lax.axis_index("dp")
    prompt_pair = prompt_kv[0]
    prompt_len, kv_cols = prompt_pair.shape[1:]
    heads_of = chunk_heads(kv_cols // HD)
    chunks = len(heads_of)
    starts = [sum(heads_of[:c]) for c in range(chunks)]
    spans = [slice(first * HD, (first + n) * HD) for first, n in zip(starts, heads_of)]
    x_peer, y_peer = own ^ X_BIT, own ^ Y_BIT
    dest, x_dest, y_dest = block_dest[own], block_dest[x_peer], block_dest[y_peer]
    meta = jnp.stack([dest ^ own, resp_len[own]]).astype(jnp.int32)

    own_keys, own_values = [], []
    remaining = prompt_pair
    for c in range(chunks):
        own_keys.append(remaining[0, :, spans[c]])
        own_values.append(remaining[1, :, spans[c]])
        remaining, _ = lax.optimization_barrier((remaining, (own_keys[c], own_values[c])))
    x_keys = [swap_with(part, "dp", X_BIT) for part in own_keys]
    y_values = [swap_with(part, "dp", Y_BIT) for part in own_values]

    full_hidden = whole_features(hidden)
    resp_kv = jnp.concatenate(
        [
            jnp.dot(full_hidden, w, preferred_element_type=jnp.float32).astype(jnp.bfloat16)
            for w in (w_key, w_value)
        ],
        axis=1,
    )

    x_values, y_keys = [], []
    held = (own_keys, own_values, x_keys, y_values)
    for c in range(chunks):
        keys, values, relay_keys, relay_values = (part[c] for part in held)
        sent = (pick(x_dest == own, values, relay_values), pick(y_dest == own, keys, relay_keys))
        x_values.append(swap_with(sent[0], "dp", X_BIT))
        y_keys.append(swap_with(sent[1], "dp", Y_BIT))
        held, _ = lax.optimization_barrier((held, sent))

    earlier = []
    key_parts, value_parts = [], []
    for c in range(chunks):
        sources = [own_keys[c], own_values[c], x_keys[c], y_keys[c], x_values[c], y_values[c]]
        *earlier, key_part, value_part = chunk_grads(
            starts[c], heads_of[c], meta, queries, out_grad, resp_kv, sources, prompt_len, earlier
        )
        key_parts.append(key_part)
        value_parts.append(value_part)
    grad_query, resp_key_grad, resp_value_grad = earlier

    flags = [dest == y_peer, x_dest == y_peer, dest == x_peer, y_dest == x_peer]
    grad_prompt = jnp.zeros(prompt_pair.shape, jnp.bfloat16)
    for c in range(chunks):
        from_x = swap_with(key_parts[c], "dp", X_BIT)
        from_y = swap_with(value_parts[c], "dp", Y_BIT)
        through_y = masked_sum(flags[0], key_parts[c], flags[1], from_x)
        through_x = masked_sum(flags[2], value_parts[c], flags[3], from_y)
        through_y, through_x = through_y.astype(jnp.bfloat16), through_x.astype(jnp.bfloat16)
        if c + 1 < chunks:
            flags = flags_after(flags, through_x, through_y)
        else:
            resp_key_grad, resp_value_grad, _ = lax.optimization_barrier(
                (resp_key_grad, resp_value_grad, (through_y, through_x))
            )
            partial_sum = jnp.einsum(
                "ic,dc->id", resp_key_grad, w_key, preferred_element_type=jnp.float32
            )
            partial_sum = partial_sum + jnp.einsum(
                "ic,dc->id", resp_value_grad, w_value, preferred_element_type=jnp.float32
            )
            grad_hidden = summed_share(partial_sum, hidden.shape[1])
        last_y = swap_with(through_y, "dp", Y_BIT)
        last_x = swap_with(through_x, "dp", X_BIT)
        key_sum = masked_sum(dest == own, key_parts[c], x_dest == own, from_x)
        value_sum = masked_sum(dest == own, value_parts[c], y_dest == own, from_y)
        key_sum = (key_sum + last_y.astype(jnp.float32)).astype(jnp.bfloat16)
        value_sum = (value_sum + last_x.astype(jnp.float32)).astype(jnp.bfloat16)
        at = starts[c] * HD
        grad_prompt = lax.dynamic_update_slice(grad_prompt, key_sum[None], (0, 0, at))
        grad_prompt = lax.dynamic_update_slice(grad_prompt, value_sum[None], (1, 0, at))
    return (grad_query, grad_hidden, grad_prompt[None])


def solution(mesh):
    return jax.shard_map(
        local,
        mesh=mesh,
        in_specs=(
            P("dp", "tensor"),
            P("dp", "tensor"),
            P("dp", "tensor"),
            P(None, "tensor"),
            P(None, "tensor"),
            P("dp", None, None, "tensor"),
            P(),
            P(),
        ),
        out_specs=(P("dp", "tensor"), P("dp", "tensor"), P("dp", None, None, "tensor")),
        check_vma=False,
    )
```

time: 759 us -> 103 us (0.14)
  waiting for transfers between devices: 293 us -> 28.6 us
  matrix products: 143 us -> 7.91 us
  local copies, waits for them, and re-layouts: 98.7 us -> 4.66 us
  starting transfers between devices: 107 us -> 18.1 us
  other arithmetic: 64 us -> 11.4 us
  between operations: 46.5 us -> 8.68 us
  Pallas kernels: 0 us -> 23.8 us
    ppermute x12 -> x18, waiting for transfers between devices: 217 us -> 28.6 us  [swap_with(): lax.ppermute(block, axis, [(i, i ^ bit) for i in range(lax.axis_size(axis...]
    ppermute x12 -> x18, starting transfers between devices: 107 us -> 18.1 us  [swap_with(): lax.ppermute(block, axis, [(i, i ^ bit) for i in range(lax.axis_size(axis...]
    dot_general x64 -> x4, matrix products: 84.5 us -> 7.91 us  [the longest x1 4.37 us: local(): jnp.einsum('ic,dc->id', resp_key_grad, w_key, preferred_element_type=jnp....]
    psum x1 -> x0, waiting for transfers between devices: 60.8 us -> none  [local(): lax.psum(partial_value.astype(jnp.bfloat16), 'tensor').astype(jnp.float32)]
    sub x12 -> x0, matrix products: 58.5 us -> none  [block_grads(): exponent = jnp.exp(scores - row_peak)]
    reshape x35 -> x0, local copies, waits for them, and re-layouts: 54.1 us -> none  [the longest x12 20.6 us: block_grads(): query_grad.astype(jnp.bfloat16).reshape(row_count, group_cols)]
    convert_element_type x14 -> x7, other arithmetic: 42.6 us -> 4.33 us  [the longest x1 1.19 us: summed_share(): return (pick(is_first, low, high) + received).astype(jnp.bfloat16)]
    pallas_call x0 -> x3, Pallas kernels: none -> 23.8 us  [the longest x2 22.5 us: chunk_grads(): pl.pallas_call(functools.partial(attention_grads_kernel, first=first, hea...]
  transfers between devices with their start and end apart: 14 -> 18, of which waited for: 8 -> 9; matrix products, arithmetic and copies ran while one was open for 4% -> 20% of each run, Pallas kernels for 0% -> 23%
where the time goes in v1:
time: 103 us
  waiting for transfers between devices  28.6 us (28%)
  Pallas kernels  23.8 us (23%)
  starting transfers between devices  18.1 us (18%)
  other arithmetic  11.4 us (11%)
  between operations  8.68 us (8%)
  matrix products  7.91 us (8%)
  local copies, waits for them, and re-layouts  4.66 us (5%)
    ppermute x18, waiting for transfers between devices, swap_with(): lax.ppermute(block, axis, [(i, i ^ bit) for i in range(lax.axis_size(axis...  28.6 us
    pallas_call x2, Pallas kernels, chunk_grads(): pl.pallas_call(functools.partial(attention_grads_kernel, first=first, hea...  22.5 us
    ppermute x18, starting transfers between devices, swap_with(): lax.ppermute(block, axis, [(i, i ^ bit) for i in range(lax.axis_size(axis...  18.1 us
    dot_general x1, matrix products, local(): jnp.einsum('ic,dc->id', resp_key_grad, w_key, preferred_element_type=jnp....  4.37 us
    select_n x4, other arithmetic, pick(): return jnp.where(flag, one, other)  3.1 us
  transfers between devices with their start and end apart: 18, of which 9 were waited for; matrix products, arithmetic and copies ran while one was open for 20% of the time, Pallas kernels for 23%

profile of v1, /device:TPU:0, one launch (start us, length us, event | category | flops | bytes accessed | tf_op | source)
XLA Modules:
  0.0 103.1 jit_solution(4162657132667984709)
XLA Ops:
  0.7 1.4 %slice_bitcast_fusion = (bf16[1024,256]{1,0:T(8,128)(2,1)S(1)}, bf16[1024,256]{1,0:T(8,128)(2,1)S(1)}) fusion(bf16[2,1024,512]{2,1,0:T(8,128)(2,1)} %bitcast.51), kind=kLoop, calls=%fused_computation.52 | loop fusion | bytes 2097152 | tf_op jit(solution)/shard_map/squeeze | solution.py:298
  2.1 3.0 %collective-permute-start.3 = (bf16[1024,256]{1,0:T(8,128)(2,1)S(1)}, bf16[1024,256]{1,0:T(8,128)(2,1)}, u32[]{:S(2)}, u32[]{:S(2)}) collective-permute-start(bf16[1024,256]{1,0:T(8,128)(2,1)S(1)} %get-tuple-element.41.own_values), channel_id=1, source_target_pairs={{0,4},{2,6},{4,0},{6,2},{8,12},{10,14},{12,8},{14,10},{16,20},{18,... | collective-permute-start | bytes 1572872 | tf_op jit(solution)/shard_map/ppermute | solution.py:21
  5.1 1.5 %collective-permute-start.2 = (bf16[1024,256]{1,0:T(8,128)(2,1)S(1)}, bf16[1024,256]{1,0:T(8,128)(2,1)}, u32[]{:S(2)}, u32[]{:S(2)}) collective-permute-start(bf16[1024,256]{1,0:T(8,128)(2,1)S(1)} %get-tuple-element.42.own_keys), channel_id=1, source_target_pairs={{0,2},{2,0},{4,6},{6,4},{8,10},{10,8},{12,14},{14,12},{16,18},{18,... | collective-permute-start | bytes 1572872 | tf_op jit(solution)/shard_map/ppermute | solution.py:21
  15.1 2.9 %collective-permute-done.3.y_values = bf16[1024,256]{1,0:T(8,128)(2,1)} collective-permute-done((bf16[1024,256]{1,0:T(8,128)(2,1)S(1)}, bf16[1024,256]{1,0:T(8,128)(2,1)}, u32[]{:S(2)}, u32[]{:S(2)}) %collective-permute-start.3) | collective-permute-done | bytes 524320 | tf_op jit(solution)/shard_map/ppermute | solution.py:21
  18.0 2.1 %collective-permute-done.2.x_keys = bf16[1024,256]{1,0:T(8,128)(2,1)} collective-permute-done((bf16[1024,256]{1,0:T(8,128)(2,1)S(1)}, bf16[1024,256]{1,0:T(8,128)(2,1)}, u32[]{:S(2)}, u32[]{:S(2)}) %collective-permute-start.2) | collective-permute-done | bytes 524320 | tf_op jit(solution)/shard_map/ppermute | solution.py:21
  20.1 1.6 %broadcast_select_fusion.5 = (bf16[1024,256]{1,0:T(8,128)(2,1)S(1)}, bf16[1024,256]{1,0:T(8,128)(2,1)S(1)}) fusion(bf16[1024,256]{1,0:T(8,128)(2,1)} %collective-permute-done.2.x_keys, pred[]{:T(512)S(6)} %eq.17, bf16[2,1024,512]{2,1,0:T(8,128)(2,1)} %bitcast.52, bf16[1024,256]{1,0:T(8,128)(2,1)} %collective-permute-done.3.y_values, pred[]{:T(512)S(6)} %eq.36), kind=kLoop, calls=%fused_computation.59 | loop fusion | flops 524288 | bytes 3145730 | tf_op jit(solution)/shard_map/jit(_where)/select_n | solution.py:244
  22.0 2.1 %collective-permute-start.8 = (bf16[1024,256]{1,0:T(8,128)(2,1)S(1)}, bf16[1024,256]{1,0:T(8,128)(2,1)S(1)}, u32[]{:S(2)}, u32[]{:S(2)}) collective-permute-start(bf16[1024,256]{1,0:T(8,128)(2,1)S(1)} %get-tuple-element.38), channel_id=1, source_target_pairs={{0,2},{2,0},{4,6},{6,4},{8,10},{10,8},{12,14},{14,12},{16,18},{18,... | collective-permute-start | bytes 1572872 | tf_op jit(solution)/shard_map/ppermute | solution.py:21
  24.0 5.1 %collective-permute-done.4.y_values = bf16[1024,256]{1,0:T(8,128)(2,1)S(1)} collective-permute-done((bf16[1024,256]{1,0:T(8,128)(2,1)S(1)}, bf16[1024,256]{1,0:T(8,128)(2,1)S(1)}, u32[]{:S(2)}, u32[]{:S(2)}) %collective-permute-start.4) | collective-permute-done | bytes 524320 | tf_op jit(solution)/shard_map/ppermute | solution.py:21
  29.1 2.1 %collective-permute-done.1.x_keys = bf16[1024,256]{1,0:T(8,128)(2,1)S(1)} collective-permute-done((bf16[1024,256]{1,0:T(8,128)(2,1)S(1)}, bf16[1024,256]{1,0:T(8,128)(2,1)S(1)}, u32[]{:S(2)}, u32[]{:S(2)}) %collective-permute-start.1) | collective-permute-done | bytes 524320 | tf_op jit(solution)/shard_map/ppermute | solution.py:21
  31.3 1.6 %collective-permute-start.6 = (bf16[1024,256]{1,0:T(8,128)(2,1)S(1)}, bf16[1024,256]{1,0:T(8,128)(2,1)S(1)}, u32[]{:S(2)}, u32[]{:S(2)}) collective-permute-start(bf16[1024,256]{1,0:T(8,128)(2,1)S(1)} %broadcast_select_fusion.2), channel_id=1, source_target_pairs={{0,2},{2,0},{4,6},{6,4},{8,10},{10,8},{12,14},{14,12},{16,18},{18,... | collective-permute-start | bytes 1572872 | tf_op jit(solution)/shard_map/ppermute | solution.py:21
  36.7 3.6 %collective-permute-done.7.y_keys = bf16[1024,256]{1,0:T(8,128)(2,1)S(1)} collective-permute-done((bf16[1024,256]{1,0:T(8,128)(2,1)S(1)}, bf16[1024,256]{1,0:T(8,128)(2,1)S(1)}, u32[]{:S(2)}, u32[]{:S(2)}) %collective-permute-start.7) | collective-permute-done | bytes 524320 | tf_op jit(solution)/shard_map/ppermute | solution.py:21
  40.3 2.1 %collective-permute-done.8.x_values = bf16[1024,256]{1,0:T(8,128)(2,1)S(1)} collective-permute-done((bf16[1024,256]{1,0:T(8,128)(2,1)S(1)}, bf16[1024,256]{1,0:T(8,128)(2,1)S(1)}, u32[]{:S(2)}, u32[]{:S(2)}) %collective-permute-start.8) | collective-permute-done | bytes 524320 | tf_op jit(solution)/shard_map/ppermute | solution.py:21
  42.5 11.2 %attention_grads.2 = (bf16[128,4096]{1,0:T(8,128)(2,1)}, bf16[128,512]{1,0:T(8,128)(2,1)S(1)}, bf16[128,512]{1,0:T(8,128)(2,1)S(1)}, bf16[1024,256]{1,0:T(8,128)(2,1)S(1)}, bf16[1024,256]{1,0:T(8,128)(2,1)S(1)}) custom-call(s32[2]{0:T(128)S(1)} %pad_add_fusion.meta_ref, bf16[128,4096]{1,0:T(8,128)(2,1)S(1)} %copy-done.6, bf16[128,4096]{1,0:T(8,128)(2,1)S(1)} %copy-done.7, ...), custom_call_target="tpu_custom_call" | custom-call | flops 6039797760 | bytes 4194304 | tf_op jit(solution)/shard_map/attention_grads/pallas_call | solution.py:177
  54.3 1.5 %collective-permute-start.10 = (bf16[1024,256]{1,0:T(8,128)(2,1)S(1)}, bf16[1024,256]{1,0:T(8,128)(2,1)S(1)}, u32[]{:S(2)}, u32[]{:S(2)}) collective-permute-start(bf16[1024,256]{1,0:T(8,128)(2,1)S(1)} %get-tuple-element.32), channel_id=1, source_target_pairs={{0,2},{2,0},{4,6},{6,4},{8,10},{10,8},{12,14},{14,12},{16,18},{18,... | collective-permute-start | bytes 1572872 | tf_op jit(solution)/shard_map/ppermute | solution.py:21
  55.8 11.3 %attention_grads.3 = (bf16[128,4096]{1,0:T(8,128)(2,1)}, bf16[128,512]{1,0:T(8,128)(2,1)S(1)}, bf16[128,512]{1,0:T(8,128)(2,1)S(1)}, bf16[1024,256]{1,0:T(8,128)(2,1)S(1)}, bf16[1024,256]{1,0:T(8,128)(2,1)S(1)}) custom-call(s32[2]{0:T(128)S(1)} %pad_add_fusion.meta_ref, ...), custom_call_target="tpu_custom_call", output_to_operand_aliasing={{0}: (10, {}), {1}: (11, {}), {2}: (12, {})} | custom-call | flops 6039797760 | bytes 4194304 | tf_op jit(solution)/shard_map/attention_grads/pallas_call | solution.py:177
  67.7 1.5 %collective-permute-start.12 = (bf16[1024,256]{1,0:T(8,128)(2,1)S(1)}, bf16[1024,256]{1,0:T(8,128)(2,1)S(1)}, u32[]{:S(2)}, u32[]{:S(2)}) collective-permute-start(bf16[1024,256]{1,0:T(8,128)(2,1)S(1)} %get-tuple-element.34), channel_id=1, source_target_pairs={{0,4},{2,6},{4,0},{6,2},{8,12},{10,14},{12,8},{14,10},{16,20},{18,... | collective-permute-start | bytes 1572872 | tf_op jit(solution)/shard_map/ppermute | solution.py:21
  70.2 1.5 %collective-permute-start.15 = (bf16[1024,256]{1,0:T(8,128)(2,1)}, bf16[1024,256]{1,0:T(8,128)(2,1)}, u32[]{:S(2)}, u32[]{:S(2)}) collective-permute-start(bf16[1024,256]{1,0:T(8,128)(2,1)} %fusion.1.x_ref), channel_id=1, source_target_pairs={{0,2},{2,0},{4,6},{6,4},{8,10},{10,8},{12,14},{14,12},{16,18},{18,... | collective-permute-start | bytes 1572872 | tf_op jit(solution)/shard_map/ppermute | solution.py:21
  74.4 1.4 %fusion.29 = (s32[1,1]{1,0:T(1,128)}, s32[1,1]{1,0:T(1,128)}, s32[1,1]{1,0:T(1,128)}, s32[1,1]{1,0:T(1,128)}) fusion(s32[8,128]{1,0:T(8,128)} %flags_after.1), kind=kLoop, calls=%fused_computation.65 | loop fusion | bytes 32 | tf_op jit(solution)/shard_map/slice | solution.py:240
  78.3 3.6 %collective-permute-done.11 = bf16[1024,256]{1,0:T(8,128)(2,1)S(1)} collective-permute-done((bf16[1024,256]{1,0:T(8,128)(2,1)S(1)}, bf16[1024,256]{1,0:T(8,128)(2,1)S(1)}, u32[]{:S(2)}, u32[]{:S(2)}) %collective-permute-start.11) | collective-permute-done | bytes 524320 | tf_op jit(solution)/shard_map/ppermute | solution.py:21
  82.2 1.6 %collective-permute-start.16 = (bf16[1024,256]{1,0:T(8,128)(2,1)S(1)}, bf16[1024,256]{1,0:T(8,128)(2,1)S(1)}, u32[]{:S(2)}, u32[]{:S(2)}) collective-permute-start(bf16[1024,256]{1,0:T(8,128)(2,1)S(1)} %fusion.11), channel_id=1, source_target_pairs={{0,4},{2,6},{4,0},{6,2},{8,12},{10,14},{12,8},{14,10},{16,20},{18,... | collective-permute-start | bytes 1572872 | tf_op jit(solution)/shard_map/ppermute | solution.py:21
  84.6 4.4 %fusion.31 = f32[128,5120]{1,0:T(8,128)S(1)} fusion(bf16[128,512]{1,0:T(8,128)(2,1)S(1)} %get-tuple-element.35, bf16[5120,512]{1,0:T(8,128)(2,1)} %param.11), kind=kOutput, calls=%fused_computation.67 | convolution fusion | flops 671088640 | bytes 7995392 | tf_op jit(solution)/shard_map/ic,dc->id/dot_general | solution.py:346
  89.0 1.8 %convolution_add_fusion = f32[128,5120]{1,0:T(8,128)S(1)} fusion(f32[128,5120]{1,0:T(8,128)S(1)} %fusion.31, bf16[128,512]{1,0:T(8,128)(2,1)S(1)} %get-tuple-element.36, bf16[5120,512]{1,0:T(8,128)(2,1)S(1)} %bitcast.50), kind=kOutput, calls=%fused_computation | convolution fusion | flops 671744000 | bytes 10616832 | tf_op jit(solution)/shard_map/ic,dc->id/dot_general | solution.py:349
  91.1 2.8 %collective-permute-done.14 = bf16[1024,256]{1,0:T(8,128)(2,1)} collective-permute-done((bf16[1024,256]{1,0:T(8,128)(2,1)}, bf16[1024,256]{1,0:T(8,128)(2,1)}, u32[]{:S(2)}, u32[]{:S(2)}) %collective-permute-start.14) | collective-permute-done | bytes 524320 | tf_op jit(solution)/shard_map/ppermute | solution.py:21
  96.8 4.2 %collective-permute-done.16 = bf16[1024,256]{1,0:T(8,128)(2,1)S(1)} collective-permute-done((bf16[1024,256]{1,0:T(8,128)(2,1)S(1)}, bf16[1024,256]{1,0:T(8,128)(2,1)S(1)}, u32[]{:S(2)}, u32[]{:S(2)}) %collective-permute-start.16) | collective-permute-done | bytes 524320 | tf_op jit(solution)/shard_map/ppermute | solution.py:21
  (94 shorter events, 18.5 us)
Async XLA Ops:
  0.7 12.5 %copy-start.20 = (s32[16]{0:T(128)S(1)}, s32[16]{0:T(128)}, u32[]{:S(2)}) copy-start(s32[16]{0:T(128)} %param.15) | copy-start | bytes 196
  2.1 19.6 %copy-start.4 = (bf16[1024,256]{1,0:T(8,128)(2,1)}, bf16[1024,256]{1,0:T(8,128)(2,1)S(1)}, u32[]{:S(2)}) copy-start(bf16[1024,256]{1,0:T(8,128)(2,1)S(1)} %get-tuple-element.42.own_keys) | copy-start | bytes 1572868
  2.1 15.9 %collective-permute-start.3 = (bf16[1024,256]{1,0:T(8,128)(2,1)S(1)}, bf16[1024,256]{1,0:T(8,128)(2,1)}, u32[]{:S(2)}, u32[]{:S(2)}) collective-permute-start(bf16[1024,256]{1,0:T(8,128)(2,1)S(1)} %get-tuple-element.41.own_values), channel_id=1, source_target_pairs={{0,4},{2,6},{4,0},{6,2},{8,12},{10,14},{12,8},{14,10},{16,20},{18,... | collective-permute-start | bytes 1572872 | tf_op jit(solution)/shard_map/ppermute | solution.py:21
  5.1 15.0 %collective-permute-start.2 = (bf16[1024,256]{1,0:T(8,128)(2,1)S(1)}, bf16[1024,256]{1,0:T(8,128)(2,1)}, u32[]{:S(2)}, u32[]{:S(2)}) collective-permute-start(bf16[1024,256]{1,0:T(8,128)(2,1)S(1)} %get-tuple-element.42.own_keys), channel_id=1, source_target_pairs={{0,2},{2,0},{4,6},{6,4},{8,10},{10,8},{12,14},{14,12},{16,18},{18,... | collective-permute-start | bytes 1572872 | tf_op jit(solution)/shard_map/ppermute | solution.py:21
  6.7 22.4 %collective-permute-start.4 = (bf16[1024,256]{1,0:T(8,128)(2,1)S(1)}, bf16[1024,256]{1,0:T(8,128)(2,1)S(1)}, u32[]{:S(2)}, u32[]{:S(2)}) collective-permute-start(bf16[1024,256]{1,0:T(8,128)(2,1)S(1)} %get-tuple-element.23.own_values), channel_id=1, source_target_pairs={{0,4},{2,6},{4,0},{6,2},{8,12},{10,14},{12,8},{14,10},{16,20},{18,... | collective-permute-start | bytes 1572872 | tf_op jit(solution)/shard_map/ppermute | solution.py:21
  7.3 23.9 %collective-permute-start.1 = (bf16[1024,256]{1,0:T(8,128)(2,1)S(1)}, bf16[1024,256]{1,0:T(8,128)(2,1)S(1)}, u32[]{:S(2)}, u32[]{:S(2)}) collective-permute-start(bf16[1024,256]{1,0:T(8,128)(2,1)S(1)} %get-tuple-element.21.own_keys), channel_id=1, source_target_pairs={{0,2},{2,0},{4,6},{6,4},{8,10},{10,8},{12,14},{14,12},{16,18},{18,... | collective-permute-start | bytes 1572872 | tf_op jit(solution)/shard_map/ppermute | solution.py:21
  7.4 26.1 %collective-permute-start = (bf16[128,2560]{1,0:T(8,128)(2,1)}, bf16[128,2560]{1,0:T(8,128)(2,1)}, u32[]{:S(2)}, u32[]{:S(2)}) collective-permute-start(bf16[128,2560]{1,0:T(8,128)(2,1)} %param.8), channel_id=1, source_target_pairs={{0,1},{1,0},{2,3},{3,2},{4,5},{5,4},{6,7},{7,6},{8,9},{9,8},{10,11... | collective-permute-start | bytes 1966088 | tf_op jit(solution)/shard_map/ppermute | solution.py:21
  18.0 16.9 %copy-start.8 = (bf16[5120,512]{1,0:T(8,128)(2,1)S(1)}, bf16[5120,512]{1,0:T(8,128)(2,1)}, u32[]{:S(2)}) copy-start(bf16[5120,512]{1,0:T(8,128)(2,1)} %param.12) | copy-start | bytes 15728644
  20.1 15.7 %slice-start = ((s8[5242880]{0:T(1024)(128)(4,1)}), s8[4194304]{0:T(1024)(128)(4,1)S(1)}, s32[]{:S(2)}) async-start(s8[5242880]{0:T(1024)(128)(4,1)} %bitcast.47), calls=%async_computation | async-start | bytes 8388608
  21.7 18.6 %collective-permute-start.7 = (bf16[1024,256]{1,0:T(8,128)(2,1)S(1)}, bf16[1024,256]{1,0:T(8,128)(2,1)S(1)}, u32[]{:S(2)}, u32[]{:S(2)}) collective-permute-start(bf16[1024,256]{1,0:T(8,128)(2,1)S(1)} %get-tuple-element.37), channel_id=1, source_target_pairs={{0,4},{2,6},{4,0},{6,2},{8,12},{10,14},{12,8},{14,10},{16,20},{18,... | collective-permute-start | bytes 1572872 | tf_op jit(solution)/shard_map/ppermute | solution.py:21
  22.0 20.5 %collective-permute-start.8 = (bf16[1024,256]{1,0:T(8,128)(2,1)S(1)}, bf16[1024,256]{1,0:T(8,128)(2,1)S(1)}, u32[]{:S(2)}, u32[]{:S(2)}) collective-permute-start(bf16[1024,256]{1,0:T(8,128)(2,1)S(1)} %get-tuple-element.38), channel_id=1, source_target_pairs={{0,2},{2,0},{4,6},{6,4},{8,10},{10,8},{12,14},{14,12},{16,18},{18,... | collective-permute-start | bytes 1572872 | tf_op jit(solution)/shard_map/ppermute | solution.py:21
  31.3 24.5 %collective-permute-start.6 = (bf16[1024,256]{1,0:T(8,128)(2,1)S(1)}, bf16[1024,256]{1,0:T(8,128)(2,1)S(1)}, u32[]{:S(2)}, u32[]{:S(2)}) collective-permute-start(bf16[1024,256]{1,0:T(8,128)(2,1)S(1)} %broadcast_select_fusion.2), channel_id=1, source_target_pairs={{0,2},{2,0},{4,6},{6,4},{8,10},{10,8},{12,14},{14,12},{16,18},{18,... | collective-permute-start | bytes 1572872 | tf_op jit(solution)/shard_map/ppermute | solution.py:21
  32.9 22.9 %collective-permute-start.5 = (bf16[1024,256]{1,0:T(8,128)(2,1)S(1)}, bf16[1024,256]{1,0:T(8,128)(2,1)S(1)}, u32[]{:S(2)}, u32[]{:S(2)}) collective-permute-start(bf16[1024,256]{1,0:T(8,128)(2,1)S(1)} %broadcast_select_fusion.4), channel_id=1, source_target_pairs={{0,4},{2,6},{4,0},{6,2},{8,12},{10,14},{12,8},{14,10},{16,20},{18,... | collective-permute-start | bytes 1572872 | tf_op jit(solution)/shard_map/ppermute | solution.py:21
  36.7 19.1 %copy-start.1 = (bf16[1024,256]{1,0:T(8,128)(2,1)S(1)}, bf16[1024,256]{1,0:T(8,128)(2,1)}, u32[]{:S(2)}) copy-start(bf16[1024,256]{1,0:T(8,128)(2,1)} %copy-done) | copy-start | bytes 1572868
  36.7 19.1 %copy-start.3 = (bf16[1024,256]{1,0:T(8,128)(2,1)S(1)}, bf16[1024,256]{1,0:T(8,128)(2,1)}, u32[]{:S(2)}) copy-start(bf16[1024,256]{1,0:T(8,128)(2,1)} %copy-done.2) | copy-start | bytes 1572868
  53.7 15.5 %collective-permute-start.9 = (bf16[1024,256]{1,0:T(8,128)(2,1)S(1)}, bf16[1024,256]{1,0:T(8,128)(2,1)S(1)}, u32[]{:S(2)}, u32[]{:S(2)}) collective-permute-start(bf16[1024,256]{1,0:T(8,128)(2,1)S(1)} %get-tuple-element.31), channel_id=1, source_target_pairs={{0,4},{2,6},{4,0},{6,2},{8,12},{10,14},{12,8},{14,10},{16,20},{18,... | collective-permute-start | bytes 1572872 | tf_op jit(solution)/shard_map/ppermute | solution.py:21
  54.3 17.4 %collective-permute-start.10 = (bf16[1024,256]{1,0:T(8,128)(2,1)S(1)}, bf16[1024,256]{1,0:T(8,128)(2,1)S(1)}, u32[]{:S(2)}, u32[]{:S(2)}) collective-permute-start(bf16[1024,256]{1,0:T(8,128)(2,1)S(1)} %get-tuple-element.32), channel_id=1, source_target_pairs={{0,2},{2,0},{4,6},{6,4},{8,10},{10,8},{12,14},{14,12},{16,18},{18,... | collective-permute-start | bytes 1572872 | tf_op jit(solution)/shard_map/ppermute | solution.py:21
  67.1 14.9 %collective-permute-start.11 = (bf16[1024,256]{1,0:T(8,128)(2,1)S(1)}, bf16[1024,256]{1,0:T(8,128)(2,1)S(1)}, u32[]{:S(2)}, u32[]{:S(2)}) collective-permute-start(bf16[1024,256]{1,0:T(8,128)(2,1)S(1)} %get-tuple-element.33), channel_id=1, source_target_pairs={{0,2},{2,0},{4,6},{6,4},{8,10},{10,8},{12,14},{14,12},{16,18},{18,... | collective-permute-start | bytes 1572872 | tf_op jit(solution)/shard_map/ppermute | solution.py:21
  67.7 16.1 %collective-permute-start.12 = (bf16[1024,256]{1,0:T(8,128)(2,1)S(1)}, bf16[1024,256]{1,0:T(8,128)(2,1)S(1)}, u32[]{:S(2)}, u32[]{:S(2)}) collective-permute-start(bf16[1024,256]{1,0:T(8,128)(2,1)S(1)} %get-tuple-element.34), channel_id=1, source_target_pairs={{0,4},{2,6},{4,0},{6,2},{8,12},{10,14},{12,8},{14,10},{16,20},{18,... | collective-permute-start | bytes 1572872 | tf_op jit(solution)/shard_map/ppermute | solution.py:21
  70.2 25.2 %collective-permute-start.15 = (bf16[1024,256]{1,0:T(8,128)(2,1)}, bf16[1024,256]{1,0:T(8,128)(2,1)}, u32[]{:S(2)}, u32[]{:S(2)}) collective-permute-start(bf16[1024,256]{1,0:T(8,128)(2,1)} %fusion.1.x_ref), channel_id=1, source_target_pairs={{0,2},{2,0},{4,6},{6,4},{8,10},{10,8},{12,14},{14,12},{16,18},{18,... | collective-permute-start | bytes 1572872 | tf_op jit(solution)/shard_map/ppermute | solution.py:21
  72.7 21.2 %collective-permute-start.14 = (bf16[1024,256]{1,0:T(8,128)(2,1)}, bf16[1024,256]{1,0:T(8,128)(2,1)}, u32[]{:S(2)}, u32[]{:S(2)}) collective-permute-start(bf16[1024,256]{1,0:T(8,128)(2,1)} %fusion.6.y_ref), channel_id=1, source_target_pairs={{0,4},{2,6},{4,0},{6,2},{8,12},{10,14},{12,8},{14,10},{16,20},{18,... | collective-permute-start | bytes 1572872 | tf_op jit(solution)/shard_map/ppermute | solution.py:21
  82.2 18.8 %collective-permute-start.16 = (bf16[1024,256]{1,0:T(8,128)(2,1)S(1)}, bf16[1024,256]{1,0:T(8,128)(2,1)S(1)}, u32[]{:S(2)}, u32[]{:S(2)}) collective-permute-start(bf16[1024,256]{1,0:T(8,128)(2,1)S(1)} %fusion.11), channel_id=1, source_target_pairs={{0,4},{2,6},{4,0},{6,2},{8,12},{10,14},{12,8},{14,10},{16,20},{18,... | collective-permute-start | bytes 1572872 | tf_op jit(solution)/shard_map/ppermute | solution.py:21
  84.0 17.3 %collective-permute-start.17 = (bf16[1024,256]{1,0:T(8,128)(2,1)S(1)}, bf16[1024,256]{1,0:T(8,128)(2,1)S(1)}, u32[]{:S(2)}, u32[]{:S(2)}) collective-permute-start(bf16[1024,256]{1,0:T(8,128)(2,1)S(1)} %fusion.16), channel_id=1, source_target_pairs={{0,2},{2,0},{4,6},{6,4},{8,10},{10,8},{12,14},{14,12},{16,18},{18,... | collective-permute-start | bytes 1572872 | tf_op jit(solution)/shard_map/ppermute | solution.py:21
  91.0 10.6 %collective-permute-start.13 = (bf16[128,2560]{1,0:T(8,128)(2,1)S(1)}, bf16[128,2560]{1,0:T(8,128)(2,1)S(1)}, u32[]{:S(2)}, u32[]{:S(2)}) collective-permute-start(bf16[128,2560]{1,0:T(8,128)(2,1)S(1)} %select_convert_fusion), channel_id=1, source_target_pairs={{0,1},{1,0},{2,3},{3,2},{4,5},{5,4},{6,7},{7,6},{8,9},{9,8},{10,11... | collective-permute-start | bytes 1966088 | tf_op jit(solution)/shard_map/ppermute | solution.py:21
  (19 other events, 94.6 us)

commit v2 on v1

--- a/solution.py
+++ b/solution.py
@@ -11,6 +11,7 @@
 HD = 128
 GROUP = 4
 HEADS_AT_ONCE = 2
+STRIP = 384
 X_BIT = 1
 Y_BIT = 2
 
@@ -43,10 +44,12 @@
     refs = refs[aliased:]
     outputs, refs = refs[:5], refs[5:]
     query, upstream, keys, values, keys_t, value_grad, key_grad = refs[:7]
-    results, (load_sems, store_sems) = refs[7:12], refs[12:]
+    scores, prob_grad, weights, score_grad = refs[7:11]
+    results, (load_sems, store_sems) = refs[11:16], refs[16:]
     mode = meta_ref[0]
     length = meta_ref[1]
     rows = resp_kv.shape[0]
+    key_count = prompt_len + rows
     score_scale = 1.0 / math.sqrt(HD)
     prompt_part = slice(0, prompt_len)
     resp_part = slice(prompt_len, prompt_len + rows)
@@ -108,11 +111,21 @@
         tile_query = jnp.concatenate([query[h, :, part] for part in parts], axis=0)
         tile_upstream = jnp.concatenate([upstream[h, :, part] for part in parts], axis=0)
         tile_upstream = jnp.where(live, tile_upstream, jnp.zeros((), jnp.bfloat16))
-        scores = lax.dot_general(keys[h], tile_query, nt, preferred_element_type=jnp.float32)
-        prob_grad = lax.dot_general(
-            values[h], tile_upstream, nt, preferred_element_type=jnp.float32
+        return h, parts, tile_query, tile_upstream
+
+    def put_scores(buffer, tile, strip, peak):
+        part = lax.dot_general(keys[tile[0], strip], tile[2], nt, preferred_element_type=jnp.float32)
+        if strip.stop == key_count:
+            resp_scores = jnp.where(visible, part[-rows:], big_negative)
+            part = jnp.concatenate([part[:-rows], resp_scores], axis=0)
+        scores[buffer, strip] = part
+        part_peak = jnp.max(part, axis=0, keepdims=True)
+        return part_peak if peak is None else jnp.maximum(peak, part_peak)
+
+    def put_prob_grad(buffer, tile, strip):
+        prob_grad[buffer, strip] = lax.dot_general(
+            values[tile[0], strip], tile[3], nt, preferred_element_type=jnp.float32
         )
-        return parts, tile_query, tile_upstream, scores, prob_grad
 
     def store(h, slot, target):
         copy = pltpu.make_async_copy(results[slot].at[h], target, store_sems.at[h, slot])
@@ -120,37 +133,54 @@
         return copy
 
     stores = []
+    strips = [slice(i, i + STRIP) for i in range(0, key_count, STRIP)]
     steps = [(h, index) for h in range(heads) for index in range(tiles)]
     following = tile_inputs(*steps[0])
+    following_peak = None
+    for strip in strips:
+        following_peak = put_scores(0, following, strip, following_peak)
+        put_prob_grad(0, following, strip)
     for step, (h, index) in enumerate(steps):
-        parts, tile_query, tile_upstream, scores, prob_grad = following
-        if step + 1 < len(steps):
-            following = tile_inputs(*steps[step + 1])
-        resp_scores = jnp.where(visible, scores[prompt_len:], big_negative)
-        scores = jnp.concatenate([scores[:prompt_len], resp_scores], axis=0)
-        peak = jnp.max(scores, axis=0, keepdims=True)
-        exponent = jnp.exp2((scores - peak) * (score_scale * math.log2(math.e)))
-        probs = exponent * (1.0 / jnp.sum(exponent, axis=0, keepdims=True))
-        weights = probs.astype(jnp.bfloat16)
-        row_dot = jnp.sum(weights.astype(jnp.float32) * prob_grad, axis=0, keepdims=True)
-        score_grad = (probs * (prob_grad - row_dot)).astype(jnp.bfloat16)
-        value_term = jnp.dot(weights, tile_upstream, preferred_element_type=jnp.float32)
-        key_term = jnp.dot(score_grad, tile_query, preferred_element_type=jnp.float32)
-        query_grad_t = jnp.dot(keys_t[h], score_grad, preferred_element_type=jnp.float32)
+        now, later = step % 2, (step + 1) % 2
+        (_, parts, tile_query, tile_upstream), peak = following, following_peak
+        more = step + 1 < len(steps)
+        if more:
+            following, following_peak = tile_inputs(*steps[step + 1]), None
+        total = jnp.zeros((1, scores.shape[2]), jnp.float32)
+        for strip in strips:
+            if more:
+                following_peak = put_scores(later, following, strip, following_peak)
+            exponent = (scores[now, strip] - peak) * (score_scale * math.log2(math.e))
+            exponent = jnp.exp2(exponent)
+            scores[now, strip] = exponent
+            total += jnp.sum(exponent, axis=0, keepdims=True)
+        inverse = 1.0 / total
+        row_dot = jnp.zeros_like(total)
+        for strip in strips:
+            if more:
+                put_prob_grad(later, following, strip)
+            part = (scores[now, strip] * inverse).astype(jnp.bfloat16)
+            weights[strip] = part
+            part = part.astype(jnp.float32) * prob_grad[now, strip]
+            row_dot += jnp.sum(part, axis=0, keepdims=True)
+        for strip in strips:
+            part = scores[now, strip] * inverse * (prob_grad[now, strip] - row_dot)
+            part = part.astype(jnp.bfloat16)
+            score_grad[strip] = part
+            value_term = jnp.dot(weights[strip], tile_upstream, preferred_element_type=jnp.float32)
+            key_term = jnp.dot(part, tile_query, preferred_element_type=jnp.float32)
+            value_grad[strip] = value_grad[strip] + value_term if index > 0 else value_term
+            key_grad[strip] = key_grad[strip] + key_term if index > 0 else key_term
+        query_grad_t = jnp.dot(keys_t[h], score_grad[...], preferred_element_type=jnp.float32)
         query_grad = (query_grad_t * score_scale).T.astype(jnp.bfloat16)
         for k, part in enumerate(parts):
             results[0][h, :, part] = query_grad[k * rows : (k + 1) * rows]
-        if index > 0:
-            value_term = value_grad[...] + value_term
-            key_term = key_grad[...] + key_term
         if index + 1 < tiles:
-            value_grad[...] = value_term
-            key_grad[...] = key_term
             continue
-        value_term = value_term.astype(jnp.bfloat16)
+        value_term = value_grad[...].astype(jnp.bfloat16)
         results[2][h] = value_term[resp_part]
         results[4][h] = value_term[prompt_part]
-        key_term = (key_term * score_scale).astype(jnp.bfloat16)
+        key_term = (key_grad[...] * score_scale).astype(jnp.bfloat16)
         results[1][h] = key_term[resp_part]
         results[3][h] = key_term[prompt_part]
         stores += [
@@ -194,6 +224,10 @@
             pltpu.VMEM((heads, HD, key_count), bf16),
             pltpu.VMEM((key_count, HD), jnp.float32),
             pltpu.VMEM((key_count, HD), jnp.float32),
+            pltpu.VMEM((2, key_count, HEADS_AT_ONCE * rows), jnp.float32),
+            pltpu.VMEM((2, key_count, HEADS_AT_ONCE * rows), jnp.float32),
+            pltpu.VMEM((key_count, HEADS_AT_ONCE * rows), bf16),
+            pltpu.VMEM((key_count, HEADS_AT_ONCE * rows), bf16),
             pltpu.VMEM((heads, rows, group_cols), bf16),
             pltpu.VMEM((heads, rows, HD), bf16),
             pltpu.VMEM((heads, rows, HD), bf16),

time: 103 us -> 103 us (level)
  no operation moved by 1% of the time
where the time goes in v2:
time: 103 us
  waiting for transfers between devices  28.2 us (27%)
  Pallas kernels  23.8 us (23%)
  starting transfers between devices  18 us (17%)
  other arithmetic  11.5 us (11%)
  between operations  8.7 us (8%)
  matrix products  7.91 us (8%)
  local copies, waits for them, and re-layouts  4.66 us (5%)
    ppermute x18, waiting for transfers between devices, swap_with(): lax.ppermute(block, axis, [(i, i ^ bit) for i in range(lax.axis_size(axis...  28.2 us
    pallas_call x2, Pallas kernels, chunk_grads(): pl.pallas_call(functools.partial(attention_grads_kernel, first=first, hea...  22.5 us
    ppermute x18, starting transfers between devices, swap_with(): lax.ppermute(block, axis, [(i, i ^ bit) for i in range(lax.axis_size(axis...  18 us
    dot_general x1, matrix products, local(): jnp.einsum('ic,dc->id', resp_key_grad, w_key, preferred_element_type=jnp....  4.38 us
    select_n x4, other arithmetic, pick(): return jnp.where(flag, one, other)  3.26 us
  transfers between devices with their start and end apart: 18, of which 9 were waited for; matrix products, arithmetic and copies ran while one was open for 20% of the time, Pallas kernels for 23%

profile of v2, /device:TPU:0, one launch (start us, length us, event | category | flops | bytes accessed | tf_op | source)
XLA Modules:
  0.0 102.8 jit_solution(13198903325962731865)
XLA Ops:
  0.7 1.4 %slice_bitcast_fusion = (bf16[1024,256]{1,0:T(8,128)(2,1)S(1)}, bf16[1024,256]{1,0:T(8,128)(2,1)S(1)}) fusion(bf16[2,1024,512]{2,1,0:T(8,128)(2,1)} %bitcast.51), kind=kLoop, calls=%fused_computation.52 | loop fusion | bytes 2097152 | tf_op jit(solution)/shard_map/squeeze | solution.py:332
  2.1 3.0 %collective-permute-start.3 = (bf16[1024,256]{1,0:T(8,128)(2,1)S(1)}, bf16[1024,256]{1,0:T(8,128)(2,1)}, u32[]{:S(2)}, u32[]{:S(2)}) collective-permute-start(bf16[1024,256]{1,0:T(8,128)(2,1)S(1)} %get-tuple-element.41.own_values), channel_id=1, source_target_pairs={{0,4},{2,6},{4,0},{6,2},{8,12},{10,14},{12,8},{14,10},{16,20},{18,... | collective-permute-start | bytes 1572872 | tf_op jit(solution)/shard_map/ppermute | solution.py:22
  5.1 1.5 %collective-permute-start.2 = (bf16[1024,256]{1,0:T(8,128)(2,1)S(1)}, bf16[1024,256]{1,0:T(8,128)(2,1)}, u32[]{:S(2)}, u32[]{:S(2)}) collective-permute-start(bf16[1024,256]{1,0:T(8,128)(2,1)S(1)} %get-tuple-element.42.own_keys), channel_id=1, source_target_pairs={{0,2},{2,0},{4,6},{6,4},{8,10},{10,8},{12,14},{14,12},{16,18},{18,... | collective-permute-start | bytes 1572872 | tf_op jit(solution)/shard_map/ppermute | solution.py:22
  15.1 2.9 %collective-permute-done.3.y_values = bf16[1024,256]{1,0:T(8,128)(2,1)} collective-permute-done((bf16[1024,256]{1,0:T(8,128)(2,1)S(1)}, bf16[1024,256]{1,0:T(8,128)(2,1)}, u32[]{:S(2)}, u32[]{:S(2)}) %collective-permute-start.3) | collective-permute-done | bytes 524320 | tf_op jit(solution)/shard_map/ppermute | solution.py:22
  18.0 2.1 %collective-permute-done.2.x_keys = bf16[1024,256]{1,0:T(8,128)(2,1)} collective-permute-done((bf16[1024,256]{1,0:T(8,128)(2,1)S(1)}, bf16[1024,256]{1,0:T(8,128)(2,1)}, u32[]{:S(2)}, u32[]{:S(2)}) %collective-permute-start.2) | collective-permute-done | bytes 524320 | tf_op jit(solution)/shard_map/ppermute | solution.py:22
  20.1 1.8 %broadcast_select_fusion.5 = (bf16[1024,256]{1,0:T(8,128)(2,1)S(1)}, bf16[1024,256]{1,0:T(8,128)(2,1)S(1)}) fusion(bf16[1024,256]{1,0:T(8,128)(2,1)} %collective-permute-done.2.x_keys, pred[]{:T(512)S(6)} %eq.17, bf16[2,1024,512]{2,1,0:T(8,128)(2,1)} %bitcast.52, bf16[1024,256]{1,0:T(8,128)(2,1)} %collective-permute-done.3.y_values, pred[]{:T(512)S(6)} %eq.36), kind=kLoop, calls=%fused_computation.59 | loop fusion | flops 524288 | bytes 3145730 | tf_op jit(solution)/shard_map/jit(_where)/select_n | solution.py:278
  21.9 2.1 %collective-permute-start.8 = (bf16[1024,256]{1,0:T(8,128)(2,1)S(1)}, bf16[1024,256]{1,0:T(8,128)(2,1)S(1)}, u32[]{:S(2)}, u32[]{:S(2)}) collective-permute-start(bf16[1024,256]{1,0:T(8,128)(2,1)S(1)} %get-tuple-element.38), channel_id=1, source_target_pairs={{0,2},{2,0},{4,6},{6,4},{8,10},{10,8},{12,14},{14,12},{16,18},{18,... | collective-permute-start | bytes 1572872 | tf_op jit(solution)/shard_map/ppermute | solution.py:22
  24.0 5.1 %collective-permute-done.4.y_values = bf16[1024,256]{1,0:T(8,128)(2,1)S(1)} collective-permute-done((bf16[1024,256]{1,0:T(8,128)(2,1)S(1)}, bf16[1024,256]{1,0:T(8,128)(2,1)S(1)}, u32[]{:S(2)}, u32[]{:S(2)}) %collective-permute-start.4) | collective-permute-done | bytes 524320 | tf_op jit(solution)/shard_map/ppermute | solution.py:22
  29.1 2.1 %collective-permute-done.1.x_keys = bf16[1024,256]{1,0:T(8,128)(2,1)S(1)} collective-permute-done((bf16[1024,256]{1,0:T(8,128)(2,1)S(1)}, bf16[1024,256]{1,0:T(8,128)(2,1)S(1)}, u32[]{:S(2)}, u32[]{:S(2)}) %collective-permute-start.1) | collective-permute-done | bytes 524320 | tf_op jit(solution)/shard_map/ppermute | solution.py:22
  31.3 1.6 %collective-permute-start.6 = (bf16[1024,256]{1,0:T(8,128)(2,1)S(1)}, bf16[1024,256]{1,0:T(8,128)(2,1)S(1)}, u32[]{:S(2)}, u32[]{:S(2)}) collective-permute-start(bf16[1024,256]{1,0:T(8,128)(2,1)S(1)} %broadcast_select_fusion.2), channel_id=1, source_target_pairs={{0,2},{2,0},{4,6},{6,4},{8,10},{10,8},{12,14},{14,12},{16,18},{18,... | collective-permute-start | bytes 1572872 | tf_op jit(solution)/shard_map/ppermute | solution.py:22
  33.5 1.4 %broadcast_select_fusion.1 = (bf16[128,2560]{1,0:T(8,128)(2,1)S(1)}, bf16[128,2560]{1,0:T(8,128)(2,1)S(1)}) fusion(bf16[128,2560]{1,0:T(8,128)(2,1)} %param.8, bf16[128,2560]{1,0:T(8,128)(2,1)} %collective-permute-done, pred[]{:T(512)S(6)} %eq.16), kind=kLoop, calls=%fused_computation.44 | loop fusion | flops 655360 | bytes 2621441 | tf_op jit(solution)/shard_map/jit(_where)/select_n | solution.py:278
  36.7 3.6 %collective-permute-done.7.y_keys = bf16[1024,256]{1,0:T(8,128)(2,1)S(1)} collective-permute-done((bf16[1024,256]{1,0:T(8,128)(2,1)S(1)}, bf16[1024,256]{1,0:T(8,128)(2,1)S(1)}, u32[]{:S(2)}, u32[]{:S(2)}) %collective-permute-start.7) | collective-permute-done | bytes 524320 | tf_op jit(solution)/shard_map/ppermute | solution.py:22
  40.3 2.1 %collective-permute-done.8.x_values = bf16[1024,256]{1,0:T(8,128)(2,1)S(1)} collective-permute-done((bf16[1024,256]{1,0:T(8,128)(2,1)S(1)}, bf16[1024,256]{1,0:T(8,128)(2,1)S(1)}, u32[]{:S(2)}, u32[]{:S(2)}) %collective-permute-start.8) | collective-permute-done | bytes 524320 | tf_op jit(solution)/shard_map/ppermute | solution.py:22
  42.5 11.2 %attention_grads.2 = (bf16[128,4096]{1,0:T(8,128)(2,1)}, bf16[128,512]{1,0:T(8,128)(2,1)S(1)}, bf16[128,512]{1,0:T(8,128)(2,1)S(1)}, bf16[1024,256]{1,0:T(8,128)(2,1)S(1)}, bf16[1024,256]{1,0:T(8,128)(2,1)S(1)}) custom-call(s32[2]{0:T(128)S(1)} %pad_add_fusion.meta_ref, bf16[128,4096]{1,0:T(8,128)(2,1)S(1)} %copy-done.6, bf16[128,4096]{1,0:T(8,128)(2,1)S(1)} %copy-done.7, ...), custom_call_target="tpu_custom_call" | custom-call | flops 6039797760 | bytes 4194304 | tf_op jit(solution)/shard_map/attention_grads/pallas_call | solution.py:207
  53.8 2.4 %collective-permute-start.10 = (bf16[1024,256]{1,0:T(8,128)(2,1)S(1)}, bf16[1024,256]{1,0:T(8,128)(2,1)S(1)}, u32[]{:S(2)}, u32[]{:S(2)}) collective-permute-start(bf16[1024,256]{1,0:T(8,128)(2,1)S(1)} %get-tuple-element.32), channel_id=1, source_target_pairs={{0,2},{2,0},{4,6},{6,4},{8,10},{10,8},{12,14},{14,12},{16,18},{18,... | collective-permute-start | bytes 1572872 | tf_op jit(solution)/shard_map/ppermute | solution.py:22
  56.2 11.3 %attention_grads.3 = (bf16[128,4096]{1,0:T(8,128)(2,1)}, bf16[128,512]{1,0:T(8,128)(2,1)S(1)}, bf16[128,512]{1,0:T(8,128)(2,1)S(1)}, bf16[1024,256]{1,0:T(8,128)(2,1)S(1)}, bf16[1024,256]{1,0:T(8,128)(2,1)S(1)}) custom-call(s32[2]{0:T(128)S(1)} %pad_add_fusion.meta_ref, ...), custom_call_target="tpu_custom_call", output_to_operand_aliasing={{0}: (10, {}), {1}: (11, {}), {2}: (12, {})} | custom-call | flops 6039797760 | bytes 4194304 | tf_op jit(solution)/shard_map/attention_grads/pallas_call | solution.py:207
  67.6 1.6 %collective-permute-start.12 = (bf16[1024,256]{1,0:T(8,128)(2,1)S(1)}, bf16[1024,256]{1,0:T(8,128)(2,1)S(1)}, u32[]{:S(2)}, u32[]{:S(2)}) collective-permute-start(bf16[1024,256]{1,0:T(8,128)(2,1)S(1)} %get-tuple-element.34), channel_id=1, source_target_pairs={{0,4},{2,6},{4,0},{6,2},{8,12},{10,14},{12,8},{14,10},{16,20},{18,... | collective-permute-start | bytes 1572872 | tf_op jit(solution)/shard_map/ppermute | solution.py:22
  70.2 1.5 %collective-permute-start.15 = (bf16[1024,256]{1,0:T(8,128)(2,1)}, bf16[1024,256]{1,0:T(8,128)(2,1)}, u32[]{:S(2)}, u32[]{:S(2)}) collective-permute-start(bf16[1024,256]{1,0:T(8,128)(2,1)} %fusion.1.x_ref), channel_id=1, source_target_pairs={{0,2},{2,0},{4,6},{6,4},{8,10},{10,8},{12,14},{14,12},{16,18},{18,... | collective-permute-start | bytes 1572872 | tf_op jit(solution)/shard_map/ppermute | solution.py:22
  74.9 1.4 %fusion.29 = (s32[1,1]{1,0:T(1,128)}, s32[1,1]{1,0:T(1,128)}, s32[1,1]{1,0:T(1,128)}, s32[1,1]{1,0:T(1,128)}) fusion(s32[8,128]{1,0:T(8,128)} %flags_after.1), kind=kLoop, calls=%fused_computation.65 | loop fusion | bytes 32 | tf_op jit(solution)/shard_map/slice | solution.py:274
  78.8 3.6 %collective-permute-done.11 = bf16[1024,256]{1,0:T(8,128)(2,1)S(1)} collective-permute-done((bf16[1024,256]{1,0:T(8,128)(2,1)S(1)}, bf16[1024,256]{1,0:T(8,128)(2,1)S(1)}, u32[]{:S(2)}, u32[]{:S(2)}) %collective-permute-start.11) | collective-permute-done | bytes 524320 | tf_op jit(solution)/shard_map/ppermute | solution.py:22
  84.7 4.4 %fusion.31 = f32[128,5120]{1,0:T(8,128)S(1)} fusion(bf16[128,512]{1,0:T(8,128)(2,1)S(1)} %get-tuple-element.35, bf16[5120,512]{1,0:T(8,128)(2,1)} %param.11), kind=kOutput, calls=%fused_computation.67 | convolution fusion | flops 671088640 | bytes 7995392 | tf_op jit(solution)/shard_map/ic,dc->id/dot_general | solution.py:380
  89.2 1.8 %convolution_add_fusion = f32[128,5120]{1,0:T(8,128)S(1)} fusion(f32[128,5120]{1,0:T(8,128)S(1)} %fusion.31, bf16[128,512]{1,0:T(8,128)(2,1)S(1)} %get-tuple-element.36, bf16[5120,512]{1,0:T(8,128)(2,1)S(1)} %bitcast.50), kind=kOutput, calls=%fused_computation | convolution fusion | flops 671744000 | bytes 10616832 | tf_op jit(solution)/shard_map/ic,dc->id/dot_general | solution.py:383
  91.2 2.6 %collective-permute-done.14 = bf16[1024,256]{1,0:T(8,128)(2,1)} collective-permute-done((bf16[1024,256]{1,0:T(8,128)(2,1)}, bf16[1024,256]{1,0:T(8,128)(2,1)}, u32[]{:S(2)}, u32[]{:S(2)}) %collective-permute-start.14) | collective-permute-done | bytes 524320 | tf_op jit(solution)/shard_map/ppermute | solution.py:22
  96.7 4.0 %collective-permute-done.16 = bf16[1024,256]{1,0:T(8,128)(2,1)S(1)} collective-permute-done((bf16[1024,256]{1,0:T(8,128)(2,1)S(1)}, bf16[1024,256]{1,0:T(8,128)(2,1)S(1)}, u32[]{:S(2)}, u32[]{:S(2)}) %collective-permute-start.16) | collective-permute-done | bytes 524320 | tf_op jit(solution)/shard_map/ppermute | solution.py:22
  (94 shorter events, 17.6 us)
Async XLA Ops:
  0.7 12.5 %copy-start.20 = (s32[16]{0:T(128)S(1)}, s32[16]{0:T(128)}, u32[]{:S(2)}) copy-start(s32[16]{0:T(128)} %param.15) | copy-start | bytes 196
  2.1 19.8 %copy-start.4 = (bf16[1024,256]{1,0:T(8,128)(2,1)}, bf16[1024,256]{1,0:T(8,128)(2,1)S(1)}, u32[]{:S(2)}) copy-start(bf16[1024,256]{1,0:T(8,128)(2,1)S(1)} %get-tuple-element.42.own_keys) | copy-start | bytes 1572868
  2.1 15.9 %collective-permute-start.3 = (bf16[1024,256]{1,0:T(8,128)(2,1)S(1)}, bf16[1024,256]{1,0:T(8,128)(2,1)}, u32[]{:S(2)}, u32[]{:S(2)}) collective-permute-start(bf16[1024,256]{1,0:T(8,128)(2,1)S(1)} %get-tuple-element.41.own_values), channel_id=1, source_target_pairs={{0,4},{2,6},{4,0},{6,2},{8,12},{10,14},{12,8},{14,10},{16,20},{18,... | collective-permute-start | bytes 1572872 | tf_op jit(solution)/shard_map/ppermute | solution.py:22
  5.1 15.0 %collective-permute-start.2 = (bf16[1024,256]{1,0:T(8,128)(2,1)S(1)}, bf16[1024,256]{1,0:T(8,128)(2,1)}, u32[]{:S(2)}, u32[]{:S(2)}) collective-permute-start(bf16[1024,256]{1,0:T(8,128)(2,1)S(1)} %get-tuple-element.42.own_keys), channel_id=1, source_target_pairs={{0,2},{2,0},{4,6},{6,4},{8,10},{10,8},{12,14},{14,12},{16,18},{18,... | collective-permute-start | bytes 1572872 | tf_op jit(solution)/shard_map/ppermute | solution.py:22
  6.7 22.4 %collective-permute-start.4 = (bf16[1024,256]{1,0:T(8,128)(2,1)S(1)}, bf16[1024,256]{1,0:T(8,128)(2,1)S(1)}, u32[]{:S(2)}, u32[]{:S(2)}) collective-permute-start(bf16[1024,256]{1,0:T(8,128)(2,1)S(1)} %get-tuple-element.23.own_values), channel_id=1, source_target_pairs={{0,4},{2,6},{4,0},{6,2},{8,12},{10,14},{12,8},{14,10},{16,20},{18,... | collective-permute-start | bytes 1572872 | tf_op jit(solution)/shard_map/ppermute | solution.py:22
  7.3 23.9 %collective-permute-start.1 = (bf16[1024,256]{1,0:T(8,128)(2,1)S(1)}, bf16[1024,256]{1,0:T(8,128)(2,1)S(1)}, u32[]{:S(2)}, u32[]{:S(2)}) collective-permute-start(bf16[1024,256]{1,0:T(8,128)(2,1)S(1)} %get-tuple-element.21.own_keys), channel_id=1, source_target_pairs={{0,2},{2,0},{4,6},{6,4},{8,10},{10,8},{12,14},{14,12},{16,18},{18,... | collective-permute-start | bytes 1572872 | tf_op jit(solution)/shard_map/ppermute | solution.py:22
  7.4 26.1 %collective-permute-start = (bf16[128,2560]{1,0:T(8,128)(2,1)}, bf16[128,2560]{1,0:T(8,128)(2,1)}, u32[]{:S(2)}, u32[]{:S(2)}) collective-permute-start(bf16[128,2560]{1,0:T(8,128)(2,1)} %param.8), channel_id=1, source_target_pairs={{0,1},{1,0},{2,3},{3,2},{4,5},{5,4},{6,7},{7,6},{8,9},{9,8},{10,11... | collective-permute-start | bytes 1966088 | tf_op jit(solution)/shard_map/ppermute | solution.py:22
  18.0 16.9 %copy-start.8 = (bf16[5120,512]{1,0:T(8,128)(2,1)S(1)}, bf16[5120,512]{1,0:T(8,128)(2,1)}, u32[]{:S(2)}) copy-start(bf16[5120,512]{1,0:T(8,128)(2,1)} %param.12) | copy-start | bytes 15728644
  20.1 15.7 %slice-start = ((s8[5242880]{0:T(1024)(128)(4,1)}), s8[4194304]{0:T(1024)(128)(4,1)S(1)}, s32[]{:S(2)}) async-start(s8[5242880]{0:T(1024)(128)(4,1)} %bitcast.47), calls=%async_computation | async-start | bytes 8388608
  21.9 18.5 %collective-permute-start.7 = (bf16[1024,256]{1,0:T(8,128)(2,1)S(1)}, bf16[1024,256]{1,0:T(8,128)(2,1)S(1)}, u32[]{:S(2)}, u32[]{:S(2)}) collective-permute-start(bf16[1024,256]{1,0:T(8,128)(2,1)S(1)} %get-tuple-element.37), channel_id=1, source_target_pairs={{0,4},{2,6},{4,0},{6,2},{8,12},{10,14},{12,8},{14,10},{16,20},{18,... | collective-permute-start | bytes 1572872 | tf_op jit(solution)/shard_map/ppermute | solution.py:22
  21.9 20.5 %collective-permute-start.8 = (bf16[1024,256]{1,0:T(8,128)(2,1)S(1)}, bf16[1024,256]{1,0:T(8,128)(2,1)S(1)}, u32[]{:S(2)}, u32[]{:S(2)}) collective-permute-start(bf16[1024,256]{1,0:T(8,128)(2,1)S(1)} %get-tuple-element.38), channel_id=1, source_target_pairs={{0,2},{2,0},{4,6},{6,4},{8,10},{10,8},{12,14},{14,12},{16,18},{18,... | collective-permute-start | bytes 1572872 | tf_op jit(solution)/shard_map/ppermute | solution.py:22
  31.3 24.9 %collective-permute-start.6 = (bf16[1024,256]{1,0:T(8,128)(2,1)S(1)}, bf16[1024,256]{1,0:T(8,128)(2,1)S(1)}, u32[]{:S(2)}, u32[]{:S(2)}) collective-permute-start(bf16[1024,256]{1,0:T(8,128)(2,1)S(1)} %broadcast_select_fusion.2), channel_id=1, source_target_pairs={{0,2},{2,0},{4,6},{6,4},{8,10},{10,8},{12,14},{14,12},{16,18},{18,... | collective-permute-start | bytes 1572872 | tf_op jit(solution)/shard_map/ppermute | solution.py:22
  32.9 23.3 %collective-permute-start.5 = (bf16[1024,256]{1,0:T(8,128)(2,1)S(1)}, bf16[1024,256]{1,0:T(8,128)(2,1)S(1)}, u32[]{:S(2)}, u32[]{:S(2)}) collective-permute-start(bf16[1024,256]{1,0:T(8,128)(2,1)S(1)} %broadcast_select_fusion.4), channel_id=1, source_target_pairs={{0,4},{2,6},{4,0},{6,2},{8,12},{10,14},{12,8},{14,10},{16,20},{18,... | collective-permute-start | bytes 1572872 | tf_op jit(solution)/shard_map/ppermute | solution.py:22
  36.7 19.5 %copy-start.1 = (bf16[1024,256]{1,0:T(8,128)(2,1)S(1)}, bf16[1024,256]{1,0:T(8,128)(2,1)}, u32[]{:S(2)}) copy-start(bf16[1024,256]{1,0:T(8,128)(2,1)} %copy-done) | copy-start | bytes 1572868
  36.7 19.5 %copy-start.3 = (bf16[1024,256]{1,0:T(8,128)(2,1)S(1)}, bf16[1024,256]{1,0:T(8,128)(2,1)}, u32[]{:S(2)}) copy-start(bf16[1024,256]{1,0:T(8,128)(2,1)} %copy-done.2) | copy-start | bytes 1572868
  53.7 15.5 %collective-permute-start.9 = (bf16[1024,256]{1,0:T(8,128)(2,1)S(1)}, bf16[1024,256]{1,0:T(8,128)(2,1)S(1)}, u32[]{:S(2)}, u32[]{:S(2)}) collective-permute-start(bf16[1024,256]{1,0:T(8,128)(2,1)S(1)} %get-tuple-element.31), channel_id=1, source_target_pairs={{0,4},{2,6},{4,0},{6,2},{8,12},{10,14},{12,8},{14,10},{16,20},{18,... | collective-permute-start | bytes 1572872 | tf_op jit(solution)/shard_map/ppermute | solution.py:22
  53.8 17.9 %collective-permute-start.10 = (bf16[1024,256]{1,0:T(8,128)(2,1)S(1)}, bf16[1024,256]{1,0:T(8,128)(2,1)S(1)}, u32[]{:S(2)}, u32[]{:S(2)}) collective-permute-start(bf16[1024,256]{1,0:T(8,128)(2,1)S(1)} %get-tuple-element.32), channel_id=1, source_target_pairs={{0,2},{2,0},{4,6},{6,4},{8,10},{10,8},{12,14},{14,12},{16,18},{18,... | collective-permute-start | bytes 1572872 | tf_op jit(solution)/shard_map/ppermute | solution.py:22
  67.5 14.9 %collective-permute-start.11 = (bf16[1024,256]{1,0:T(8,128)(2,1)S(1)}, bf16[1024,256]{1,0:T(8,128)(2,1)S(1)}, u32[]{:S(2)}, u32[]{:S(2)}) collective-permute-start(bf16[1024,256]{1,0:T(8,128)(2,1)S(1)} %get-tuple-element.33), channel_id=1, source_target_pairs={{0,2},{2,0},{4,6},{6,4},{8,10},{10,8},{12,14},{14,12},{16,18},{18,... | collective-permute-start | bytes 1572872 | tf_op jit(solution)/shard_map/ppermute | solution.py:22
  67.6 16.2 %collective-permute-start.12 = (bf16[1024,256]{1,0:T(8,128)(2,1)S(1)}, bf16[1024,256]{1,0:T(8,128)(2,1)S(1)}, u32[]{:S(2)}, u32[]{:S(2)}) collective-permute-start(bf16[1024,256]{1,0:T(8,128)(2,1)S(1)} %get-tuple-element.34), channel_id=1, source_target_pairs={{0,4},{2,6},{4,0},{6,2},{8,12},{10,14},{12,8},{14,10},{16,20},{18,... | collective-permute-start | bytes 1572872 | tf_op jit(solution)/shard_map/ppermute | solution.py:22
  70.2 25.1 %collective-permute-start.15 = (bf16[1024,256]{1,0:T(8,128)(2,1)}, bf16[1024,256]{1,0:T(8,128)(2,1)}, u32[]{:S(2)}, u32[]{:S(2)}) collective-permute-start(bf16[1024,256]{1,0:T(8,128)(2,1)} %fusion.1.x_ref), channel_id=1, source_target_pairs={{0,2},{2,0},{4,6},{6,4},{8,10},{10,8},{12,14},{14,12},{16,18},{18,... | collective-permute-start | bytes 1572872 | tf_op jit(solution)/shard_map/ppermute | solution.py:22
  72.7 21.2 %collective-permute-start.14 = (bf16[1024,256]{1,0:T(8,128)(2,1)}, bf16[1024,256]{1,0:T(8,128)(2,1)}, u32[]{:S(2)}, u32[]{:S(2)}) collective-permute-start(bf16[1024,256]{1,0:T(8,128)(2,1)} %fusion.6.y_ref), channel_id=1, source_target_pairs={{0,4},{2,6},{4,0},{6,2},{8,12},{10,14},{12,8},{14,10},{16,20},{18,... | collective-permute-start | bytes 1572872 | tf_op jit(solution)/shard_map/ppermute | solution.py:22
  82.6 18.0 %collective-permute-start.16 = (bf16[1024,256]{1,0:T(8,128)(2,1)S(1)}, bf16[1024,256]{1,0:T(8,128)(2,1)S(1)}, u32[]{:S(2)}, u32[]{:S(2)}) collective-permute-start(bf16[1024,256]{1,0:T(8,128)(2,1)S(1)} %fusion.11), channel_id=1, source_target_pairs={{0,4},{2,6},{4,0},{6,2},{8,12},{10,14},{12,8},{14,10},{16,20},{18,... | collective-permute-start | bytes 1572872 | tf_op jit(solution)/shard_map/ppermute | solution.py:22
  84.0 17.0 %collective-permute-start.17 = (bf16[1024,256]{1,0:T(8,128)(2,1)S(1)}, bf16[1024,256]{1,0:T(8,128)(2,1)S(1)}, u32[]{:S(2)}, u32[]{:S(2)}) collective-permute-start(bf16[1024,256]{1,0:T(8,128)(2,1)S(1)} %fusion.16), channel_id=1, source_target_pairs={{0,2},{2,0},{4,6},{6,4},{8,10},{10,8},{12,14},{14,12},{16,18},{18,... | collective-permute-start | bytes 1572872 | tf_op jit(solution)/shard_map/ppermute | solution.py:22
  91.2 10.1 %collective-permute-start.13 = (bf16[128,2560]{1,0:T(8,128)(2,1)S(1)}, bf16[128,2560]{1,0:T(8,128)(2,1)S(1)}, u32[]{:S(2)}, u32[]{:S(2)}) collective-permute-start(bf16[128,2560]{1,0:T(8,128)(2,1)S(1)} %select_convert_fusion), channel_id=1, source_target_pairs={{0,1},{1,0},{2,3},{3,2},{4,5},{5,4},{6,7},{7,6},{8,9},{9,8},{10,11... | collective-permute-start | bytes 1966088 | tf_op jit(solution)/shard_map/ppermute | solution.py:22
  (19 other events, 93.2 us)

commit v3 on v2

--- a/solution.py
+++ b/solution.py
@@ -11,7 +11,7 @@
 HD = 128
 GROUP = 4
 HEADS_AT_ONCE = 2
-STRIP = 384
+STRIP = 576
 X_BIT = 1
 Y_BIT = 2
 

time: 103 us -> 103 us (level)
  no operation moved by 1% of the time
where the time goes in v3:
time: 103 us
  waiting for transfers between devices  28.6 us (28%)
  Pallas kernels  23.6 us (23%)
  starting transfers between devices  18.2 us (18%)
  other arithmetic  11.2 us (11%)
  between operations  8.68 us (8%)
  matrix products  7.91 us (8%)
  local copies, waits for them, and re-layouts  4.66 us (5%)
    ppermute x18, waiting for transfers between devices, swap_with(): lax.ppermute(block, axis, [(i, i ^ bit) for i in range(lax.axis_size(axis...  28.6 us
    pallas_call x2, Pallas kernels, chunk_grads(): pl.pallas_call(functools.partial(attention_grads_kernel, first=first, hea...  22.4 us
    ppermute x18, starting transfers between devices, swap_with(): lax.ppermute(block, axis, [(i, i ^ bit) for i in range(lax.axis_size(axis...  18.2 us
    dot_general x1, matrix products, local(): jnp.einsum('ic,dc->id', resp_key_grad, w_key, preferred_element_type=jnp....  4.37 us
    select_n x4, other arithmetic, pick(): return jnp.where(flag, one, other)  2.94 us
  transfers between devices with their start and end apart: 18, of which 9 were waited for; matrix products, arithmetic and copies ran while one was open for 20% of the time, Pallas kernels for 23%

profile of v3, /device:TPU:0, one launch (start us, length us, event | category | flops | bytes accessed | tf_op | source)
XLA Modules:
  0.0 103.0 jit_solution(1292329671466657286)
XLA Ops:
  0.7 1.4 %slice_bitcast_fusion = (bf16[1024,256]{1,0:T(8,128)(2,1)S(1)}, bf16[1024,256]{1,0:T(8,128)(2,1)S(1)}) fusion(bf16[2,1024,512]{2,1,0:T(8,128)(2,1)} %bitcast.51), kind=kLoop, calls=%fused_computation.52 | loop fusion | bytes 2097152 | tf_op jit(solution)/shard_map/squeeze | solution.py:332
  2.1 3.0 %collective-permute-start.3 = (bf16[1024,256]{1,0:T(8,128)(2,1)S(1)}, bf16[1024,256]{1,0:T(8,128)(2,1)}, u32[]{:S(2)}, u32[]{:S(2)}) collective-permute-start(bf16[1024,256]{1,0:T(8,128)(2,1)S(1)} %get-tuple-element.41.own_values), channel_id=1, source_target_pairs={{0,4},{2,6},{4,0},{6,2},{8,12},{10,14},{12,8},{14,10},{16,20},{18,... | collective-permute-start | bytes 1572872 | tf_op jit(solution)/shard_map/ppermute | solution.py:22
  5.1 1.5 %collective-permute-start.2 = (bf16[1024,256]{1,0:T(8,128)(2,1)S(1)}, bf16[1024,256]{1,0:T(8,128)(2,1)}, u32[]{:S(2)}, u32[]{:S(2)}) collective-permute-start(bf16[1024,256]{1,0:T(8,128)(2,1)S(1)} %get-tuple-element.42.own_keys), channel_id=1, source_target_pairs={{0,2},{2,0},{4,6},{6,4},{8,10},{10,8},{12,14},{14,12},{16,18},{18,... | collective-permute-start | bytes 1572872 | tf_op jit(solution)/shard_map/ppermute | solution.py:22
  15.1 2.9 %collective-permute-done.3.y_values = bf16[1024,256]{1,0:T(8,128)(2,1)} collective-permute-done((bf16[1024,256]{1,0:T(8,128)(2,1)S(1)}, bf16[1024,256]{1,0:T(8,128)(2,1)}, u32[]{:S(2)}, u32[]{:S(2)}) %collective-permute-start.3) | collective-permute-done | bytes 524320 | tf_op jit(solution)/shard_map/ppermute | solution.py:22
  18.0 2.1 %collective-permute-done.2.x_keys = bf16[1024,256]{1,0:T(8,128)(2,1)} collective-permute-done((bf16[1024,256]{1,0:T(8,128)(2,1)S(1)}, bf16[1024,256]{1,0:T(8,128)(2,1)}, u32[]{:S(2)}, u32[]{:S(2)}) %collective-permute-start.2) | collective-permute-done | bytes 524320 | tf_op jit(solution)/shard_map/ppermute | solution.py:22
  20.1 1.5 %broadcast_select_fusion.5 = (bf16[1024,256]{1,0:T(8,128)(2,1)S(1)}, bf16[1024,256]{1,0:T(8,128)(2,1)S(1)}) fusion(bf16[1024,256]{1,0:T(8,128)(2,1)} %collective-permute-done.2.x_keys, pred[]{:T(512)S(6)} %eq.17, bf16[2,1024,512]{2,1,0:T(8,128)(2,1)} %bitcast.52, bf16[1024,256]{1,0:T(8,128)(2,1)} %collective-permute-done.3.y_values, pred[]{:T(512)S(6)} %eq.36), kind=kLoop, calls=%fused_computation.59 | loop fusion | flops 524288 | bytes 3145730 | tf_op jit(solution)/shard_map/jit(_where)/select_n | solution.py:278
  22.0 2.1 %collective-permute-start.8 = (bf16[1024,256]{1,0:T(8,128)(2,1)S(1)}, bf16[1024,256]{1,0:T(8,128)(2,1)S(1)}, u32[]{:S(2)}, u32[]{:S(2)}) collective-permute-start(bf16[1024,256]{1,0:T(8,128)(2,1)S(1)} %get-tuple-element.38), channel_id=1, source_target_pairs={{0,2},{2,0},{4,6},{6,4},{8,10},{10,8},{12,14},{14,12},{16,18},{18,... | collective-permute-start | bytes 1572872 | tf_op jit(solution)/shard_map/ppermute | solution.py:22
  24.0 5.1 %collective-permute-done.4.y_values = bf16[1024,256]{1,0:T(8,128)(2,1)S(1)} collective-permute-done((bf16[1024,256]{1,0:T(8,128)(2,1)S(1)}, bf16[1024,256]{1,0:T(8,128)(2,1)S(1)}, u32[]{:S(2)}, u32[]{:S(2)}) %collective-permute-start.4) | collective-permute-done | bytes 524320 | tf_op jit(solution)/shard_map/ppermute | solution.py:22
  29.1 2.1 %collective-permute-done.1.x_keys = bf16[1024,256]{1,0:T(8,128)(2,1)S(1)} collective-permute-done((bf16[1024,256]{1,0:T(8,128)(2,1)S(1)}, bf16[1024,256]{1,0:T(8,128)(2,1)S(1)}, u32[]{:S(2)}, u32[]{:S(2)}) %collective-permute-start.1) | collective-permute-done | bytes 524320 | tf_op jit(solution)/shard_map/ppermute | solution.py:22
  31.3 1.6 %collective-permute-start.6 = (bf16[1024,256]{1,0:T(8,128)(2,1)S(1)}, bf16[1024,256]{1,0:T(8,128)(2,1)S(1)}, u32[]{:S(2)}, u32[]{:S(2)}) collective-permute-start(bf16[1024,256]{1,0:T(8,128)(2,1)S(1)} %broadcast_select_fusion.2), channel_id=1, source_target_pairs={{0,2},{2,0},{4,6},{6,4},{8,10},{10,8},{12,14},{14,12},{16,18},{18,... | collective-permute-start | bytes 1572872 | tf_op jit(solution)/shard_map/ppermute | solution.py:22
  36.7 3.6 %collective-permute-done.7.y_keys = bf16[1024,256]{1,0:T(8,128)(2,1)S(1)} collective-permute-done((bf16[1024,256]{1,0:T(8,128)(2,1)S(1)}, bf16[1024,256]{1,0:T(8,128)(2,1)S(1)}, u32[]{:S(2)}, u32[]{:S(2)}) %collective-permute-start.7) | collective-permute-done | bytes 524320 | tf_op jit(solution)/shard_map/ppermute | solution.py:22
  40.3 2.1 %collective-permute-done.8.x_values = bf16[1024,256]{1,0:T(8,128)(2,1)S(1)} collective-permute-done((bf16[1024,256]{1,0:T(8,128)(2,1)S(1)}, bf16[1024,256]{1,0:T(8,128)(2,1)S(1)}, u32[]{:S(2)}, u32[]{:S(2)}) %collective-permute-start.8) | collective-permute-done | bytes 524320 | tf_op jit(solution)/shard_map/ppermute | solution.py:22
  42.5 11.2 %attention_grads.2 = (bf16[128,4096]{1,0:T(8,128)(2,1)}, bf16[128,512]{1,0:T(8,128)(2,1)S(1)}, bf16[128,512]{1,0:T(8,128)(2,1)S(1)}, bf16[1024,256]{1,0:T(8,128)(2,1)S(1)}, bf16[1024,256]{1,0:T(8,128)(2,1)S(1)}) custom-call(s32[2]{0:T(128)S(1)} %pad_add_fusion.meta_ref, bf16[128,4096]{1,0:T(8,128)(2,1)S(1)} %copy-done.6, bf16[128,4096]{1,0:T(8,128)(2,1)S(1)} %copy-done.7, ...), custom_call_target="tpu_custom_call" | custom-call | flops 6039797760 | bytes 4194304 | tf_op jit(solution)/shard_map/attention_grads/pallas_call | solution.py:207
  54.2 1.5 %collective-permute-start.10 = (bf16[1024,256]{1,0:T(8,128)(2,1)S(1)}, bf16[1024,256]{1,0:T(8,128)(2,1)S(1)}, u32[]{:S(2)}, u32[]{:S(2)}) collective-permute-start(bf16[1024,256]{1,0:T(8,128)(2,1)S(1)} %get-tuple-element.32), channel_id=1, source_target_pairs={{0,2},{2,0},{4,6},{6,4},{8,10},{10,8},{12,14},{14,12},{16,18},{18,... | collective-permute-start | bytes 1572872 | tf_op jit(solution)/shard_map/ppermute | solution.py:22
  55.7 11.2 %attention_grads.3 = (bf16[128,4096]{1,0:T(8,128)(2,1)}, bf16[128,512]{1,0:T(8,128)(2,1)S(1)}, bf16[128,512]{1,0:T(8,128)(2,1)S(1)}, bf16[1024,256]{1,0:T(8,128)(2,1)S(1)}, bf16[1024,256]{1,0:T(8,128)(2,1)S(1)}) custom-call(s32[2]{0:T(128)S(1)} %pad_add_fusion.meta_ref, ...), custom_call_target="tpu_custom_call", output_to_operand_aliasing={{0}: (10, {}), {1}: (11, {}), {2}: (12, {})} | custom-call | flops 6039797760 | bytes 4194304 | tf_op jit(solution)/shard_map/attention_grads/pallas_call | solution.py:207
  67.6 1.5 %collective-permute-start.12 = (bf16[1024,256]{1,0:T(8,128)(2,1)S(1)}, bf16[1024,256]{1,0:T(8,128)(2,1)S(1)}, u32[]{:S(2)}, u32[]{:S(2)}) collective-permute-start(bf16[1024,256]{1,0:T(8,128)(2,1)S(1)} %get-tuple-element.34), channel_id=1, source_target_pairs={{0,4},{2,6},{4,0},{6,2},{8,12},{10,14},{12,8},{14,10},{16,20},{18,... | collective-permute-start | bytes 1572872 | tf_op jit(solution)/shard_map/ppermute | solution.py:22
  70.0 1.9 %collective-permute-start.15 = (bf16[1024,256]{1,0:T(8,128)(2,1)}, bf16[1024,256]{1,0:T(8,128)(2,1)}, u32[]{:S(2)}, u32[]{:S(2)}) collective-permute-start(bf16[1024,256]{1,0:T(8,128)(2,1)} %fusion.1.x_ref), channel_id=1, source_target_pairs={{0,2},{2,0},{4,6},{6,4},{8,10},{10,8},{12,14},{14,12},{16,18},{18,... | collective-permute-start | bytes 1572872 | tf_op jit(solution)/shard_map/ppermute | solution.py:22
  74.3 1.4 %fusion.29 = (s32[1,1]{1,0:T(1,128)}, s32[1,1]{1,0:T(1,128)}, s32[1,1]{1,0:T(1,128)}, s32[1,1]{1,0:T(1,128)}) fusion(s32[8,128]{1,0:T(8,128)} %flags_after.1), kind=kLoop, calls=%fused_computation.65 | loop fusion | bytes 32 | tf_op jit(solution)/shard_map/slice | solution.py:274
  78.2 3.6 %collective-permute-done.11 = bf16[1024,256]{1,0:T(8,128)(2,1)S(1)} collective-permute-done((bf16[1024,256]{1,0:T(8,128)(2,1)S(1)}, bf16[1024,256]{1,0:T(8,128)(2,1)S(1)}, u32[]{:S(2)}, u32[]{:S(2)}) %collective-permute-start.11) | collective-permute-done | bytes 524320 | tf_op jit(solution)/shard_map/ppermute | solution.py:22
  82.1 2.0 %collective-permute-start.16 = (bf16[1024,256]{1,0:T(8,128)(2,1)S(1)}, bf16[1024,256]{1,0:T(8,128)(2,1)S(1)}, u32[]{:S(2)}, u32[]{:S(2)}) collective-permute-start(bf16[1024,256]{1,0:T(8,128)(2,1)S(1)} %fusion.11), channel_id=1, source_target_pairs={{0,4},{2,6},{4,0},{6,2},{8,12},{10,14},{12,8},{14,10},{16,20},{18,... | collective-permute-start | bytes 1572872 | tf_op jit(solution)/shard_map/ppermute | solution.py:22
  84.4 4.4 %fusion.31 = f32[128,5120]{1,0:T(8,128)S(1)} fusion(bf16[128,512]{1,0:T(8,128)(2,1)S(1)} %get-tuple-element.35, bf16[5120,512]{1,0:T(8,128)(2,1)} %param.11), kind=kOutput, calls=%fused_computation.67 | convolution fusion | flops 671088640 | bytes 7995392 | tf_op jit(solution)/shard_map/ic,dc->id/dot_general | solution.py:380
  88.9 1.8 %convolution_add_fusion = f32[128,5120]{1,0:T(8,128)S(1)} fusion(f32[128,5120]{1,0:T(8,128)S(1)} %fusion.31, bf16[128,512]{1,0:T(8,128)(2,1)S(1)} %get-tuple-element.36, bf16[5120,512]{1,0:T(8,128)(2,1)S(1)} %bitcast.50), kind=kOutput, calls=%fused_computation | convolution fusion | flops 671744000 | bytes 10616832 | tf_op jit(solution)/shard_map/ic,dc->id/dot_general | solution.py:383
  91.0 2.8 %collective-permute-done.14 = bf16[1024,256]{1,0:T(8,128)(2,1)} collective-permute-done((bf16[1024,256]{1,0:T(8,128)(2,1)}, bf16[1024,256]{1,0:T(8,128)(2,1)}, u32[]{:S(2)}, u32[]{:S(2)}) %collective-permute-start.14) | collective-permute-done | bytes 524320 | tf_op jit(solution)/shard_map/ppermute | solution.py:22
  96.6 4.2 %collective-permute-done.16 = bf16[1024,256]{1,0:T(8,128)(2,1)S(1)} collective-permute-done((bf16[1024,256]{1,0:T(8,128)(2,1)S(1)}, bf16[1024,256]{1,0:T(8,128)(2,1)S(1)}, u32[]{:S(2)}, u32[]{:S(2)}) %collective-permute-start.16) | collective-permute-done | bytes 524320 | tf_op jit(solution)/shard_map/ppermute | solution.py:22
  (94 shorter events, 17.8 us)
Async XLA Ops:
  0.7 12.5 %copy-start.20 = (s32[16]{0:T(128)S(1)}, s32[16]{0:T(128)}, u32[]{:S(2)}) copy-start(s32[16]{0:T(128)} %param.15) | copy-start | bytes 196
  2.1 19.5 %copy-start.4 = (bf16[1024,256]{1,0:T(8,128)(2,1)}, bf16[1024,256]{1,0:T(8,128)(2,1)S(1)}, u32[]{:S(2)}) copy-start(bf16[1024,256]{1,0:T(8,128)(2,1)S(1)} %get-tuple-element.42.own_keys) | copy-start | bytes 1572868
  2.1 15.9 %collective-permute-start.3 = (bf16[1024,256]{1,0:T(8,128)(2,1)S(1)}, bf16[1024,256]{1,0:T(8,128)(2,1)}, u32[]{:S(2)}, u32[]{:S(2)}) collective-permute-start(bf16[1024,256]{1,0:T(8,128)(2,1)S(1)} %get-tuple-element.41.own_values), channel_id=1, source_target_pairs={{0,4},{2,6},{4,0},{6,2},{8,12},{10,14},{12,8},{14,10},{16,20},{18,... | collective-permute-start | bytes 1572872 | tf_op jit(solution)/shard_map/ppermute | solution.py:22
  5.1 15.0 %collective-permute-start.2 = (bf16[1024,256]{1,0:T(8,128)(2,1)S(1)}, bf16[1024,256]{1,0:T(8,128)(2,1)}, u32[]{:S(2)}, u32[]{:S(2)}) collective-permute-start(bf16[1024,256]{1,0:T(8,128)(2,1)S(1)} %get-tuple-element.42.own_keys), channel_id=1, source_target_pairs={{0,2},{2,0},{4,6},{6,4},{8,10},{10,8},{12,14},{14,12},{16,18},{18,... | collective-permute-start | bytes 1572872 | tf_op jit(solution)/shard_map/ppermute | solution.py:22
  6.7 22.4 %collective-permute-start.4 = (bf16[1024,256]{1,0:T(8,128)(2,1)S(1)}, bf16[1024,256]{1,0:T(8,128)(2,1)S(1)}, u32[]{:S(2)}, u32[]{:S(2)}) collective-permute-start(bf16[1024,256]{1,0:T(8,128)(2,1)S(1)} %get-tuple-element.23.own_values), channel_id=1, source_target_pairs={{0,4},{2,6},{4,0},{6,2},{8,12},{10,14},{12,8},{14,10},{16,20},{18,... | collective-permute-start | bytes 1572872 | tf_op jit(solution)/shard_map/ppermute | solution.py:22
  7.3 23.9 %collective-permute-start.1 = (bf16[1024,256]{1,0:T(8,128)(2,1)S(1)}, bf16[1024,256]{1,0:T(8,128)(2,1)S(1)}, u32[]{:S(2)}, u32[]{:S(2)}) collective-permute-start(bf16[1024,256]{1,0:T(8,128)(2,1)S(1)} %get-tuple-element.21.own_keys), channel_id=1, source_target_pairs={{0,2},{2,0},{4,6},{6,4},{8,10},{10,8},{12,14},{14,12},{16,18},{18,... | collective-permute-start | bytes 1572872 | tf_op jit(solution)/shard_map/ppermute | solution.py:22
  7.4 26.1 %collective-permute-start = (bf16[128,2560]{1,0:T(8,128)(2,1)}, bf16[128,2560]{1,0:T(8,128)(2,1)}, u32[]{:S(2)}, u32[]{:S(2)}) collective-permute-start(bf16[128,2560]{1,0:T(8,128)(2,1)} %param.8), channel_id=1, source_target_pairs={{0,1},{1,0},{2,3},{3,2},{4,5},{5,4},{6,7},{7,6},{8,9},{9,8},{10,11... | collective-permute-start | bytes 1966088 | tf_op jit(solution)/shard_map/ppermute | solution.py:22
  18.0 16.9 %copy-start.8 = (bf16[5120,512]{1,0:T(8,128)(2,1)S(1)}, bf16[5120,512]{1,0:T(8,128)(2,1)}, u32[]{:S(2)}) copy-start(bf16[5120,512]{1,0:T(8,128)(2,1)} %param.12) | copy-start | bytes 15728644
  20.1 15.7 %slice-start = ((s8[5242880]{0:T(1024)(128)(4,1)}), s8[4194304]{0:T(1024)(128)(4,1)S(1)}, s32[]{:S(2)}) async-start(s8[5242880]{0:T(1024)(128)(4,1)} %bitcast.47), calls=%async_computation | async-start | bytes 8388608
  21.6 18.8 %collective-permute-start.7 = (bf16[1024,256]{1,0:T(8,128)(2,1)S(1)}, bf16[1024,256]{1,0:T(8,128)(2,1)S(1)}, u32[]{:S(2)}, u32[]{:S(2)}) collective-permute-start(bf16[1024,256]{1,0:T(8,128)(2,1)S(1)} %get-tuple-element.37), channel_id=1, source_target_pairs={{0,4},{2,6},{4,0},{6,2},{8,12},{10,14},{12,8},{14,10},{16,20},{18,... | collective-permute-start | bytes 1572872 | tf_op jit(solution)/shard_map/ppermute | solution.py:22
  22.0 20.5 %collective-permute-start.8 = (bf16[1024,256]{1,0:T(8,128)(2,1)S(1)}, bf16[1024,256]{1,0:T(8,128)(2,1)S(1)}, u32[]{:S(2)}, u32[]{:S(2)}) collective-permute-start(bf16[1024,256]{1,0:T(8,128)(2,1)S(1)} %get-tuple-element.38), channel_id=1, source_target_pairs={{0,2},{2,0},{4,6},{6,4},{8,10},{10,8},{12,14},{14,12},{16,18},{18,... | collective-permute-start | bytes 1572872 | tf_op jit(solution)/shard_map/ppermute | solution.py:22
  31.3 24.4 %collective-permute-start.6 = (bf16[1024,256]{1,0:T(8,128)(2,1)S(1)}, bf16[1024,256]{1,0:T(8,128)(2,1)S(1)}, u32[]{:S(2)}, u32[]{:S(2)}) collective-permute-start(bf16[1024,256]{1,0:T(8,128)(2,1)S(1)} %broadcast_select_fusion.2), channel_id=1, source_target_pairs={{0,2},{2,0},{4,6},{6,4},{8,10},{10,8},{12,14},{14,12},{16,18},{18,... | collective-permute-start | bytes 1572872 | tf_op jit(solution)/shard_map/ppermute | solution.py:22
  32.9 22.8 %collective-permute-start.5 = (bf16[1024,256]{1,0:T(8,128)(2,1)S(1)}, bf16[1024,256]{1,0:T(8,128)(2,1)S(1)}, u32[]{:S(2)}, u32[]{:S(2)}) collective-permute-start(bf16[1024,256]{1,0:T(8,128)(2,1)S(1)} %broadcast_select_fusion.4), channel_id=1, source_target_pairs={{0,4},{2,6},{4,0},{6,2},{8,12},{10,14},{12,8},{14,10},{16,20},{18,... | collective-permute-start | bytes 1572872 | tf_op jit(solution)/shard_map/ppermute | solution.py:22
  36.7 19.0 %copy-start.1 = (bf16[1024,256]{1,0:T(8,128)(2,1)S(1)}, bf16[1024,256]{1,0:T(8,128)(2,1)}, u32[]{:S(2)}) copy-start(bf16[1024,256]{1,0:T(8,128)(2,1)} %copy-done) | copy-start | bytes 1572868
  36.7 19.0 %copy-start.3 = (bf16[1024,256]{1,0:T(8,128)(2,1)S(1)}, bf16[1024,256]{1,0:T(8,128)(2,1)}, u32[]{:S(2)}) copy-start(bf16[1024,256]{1,0:T(8,128)(2,1)} %copy-done.2) | copy-start | bytes 1572868
  53.6 15.4 %collective-permute-start.9 = (bf16[1024,256]{1,0:T(8,128)(2,1)S(1)}, bf16[1024,256]{1,0:T(8,128)(2,1)S(1)}, u32[]{:S(2)}, u32[]{:S(2)}) collective-permute-start(bf16[1024,256]{1,0:T(8,128)(2,1)S(1)} %get-tuple-element.31), channel_id=1, source_target_pairs={{0,4},{2,6},{4,0},{6,2},{8,12},{10,14},{12,8},{14,10},{16,20},{18,... | collective-permute-start | bytes 1572872 | tf_op jit(solution)/shard_map/ppermute | solution.py:22
  54.2 17.7 %collective-permute-start.10 = (bf16[1024,256]{1,0:T(8,128)(2,1)S(1)}, bf16[1024,256]{1,0:T(8,128)(2,1)S(1)}, u32[]{:S(2)}, u32[]{:S(2)}) collective-permute-start(bf16[1024,256]{1,0:T(8,128)(2,1)S(1)} %get-tuple-element.32), channel_id=1, source_target_pairs={{0,2},{2,0},{4,6},{6,4},{8,10},{10,8},{12,14},{14,12},{16,18},{18,... | collective-permute-start | bytes 1572872 | tf_op jit(solution)/shard_map/ppermute | solution.py:22
  66.9 14.9 %collective-permute-start.11 = (bf16[1024,256]{1,0:T(8,128)(2,1)S(1)}, bf16[1024,256]{1,0:T(8,128)(2,1)S(1)}, u32[]{:S(2)}, u32[]{:S(2)}) collective-permute-start(bf16[1024,256]{1,0:T(8,128)(2,1)S(1)} %get-tuple-element.33), channel_id=1, source_target_pairs={{0,2},{2,0},{4,6},{6,4},{8,10},{10,8},{12,14},{14,12},{16,18},{18,... | collective-permute-start | bytes 1572872 | tf_op jit(solution)/shard_map/ppermute | solution.py:22
  67.6 16.5 %collective-permute-start.12 = (bf16[1024,256]{1,0:T(8,128)(2,1)S(1)}, bf16[1024,256]{1,0:T(8,128)(2,1)S(1)}, u32[]{:S(2)}, u32[]{:S(2)}) collective-permute-start(bf16[1024,256]{1,0:T(8,128)(2,1)S(1)} %get-tuple-element.34), channel_id=1, source_target_pairs={{0,4},{2,6},{4,0},{6,2},{8,12},{10,14},{12,8},{14,10},{16,20},{18,... | collective-permute-start | bytes 1572872 | tf_op jit(solution)/shard_map/ppermute | solution.py:22
  70.0 25.2 %collective-permute-start.15 = (bf16[1024,256]{1,0:T(8,128)(2,1)}, bf16[1024,256]{1,0:T(8,128)(2,1)}, u32[]{:S(2)}, u32[]{:S(2)}) collective-permute-start(bf16[1024,256]{1,0:T(8,128)(2,1)} %fusion.1.x_ref), channel_id=1, source_target_pairs={{0,2},{2,0},{4,6},{6,4},{8,10},{10,8},{12,14},{14,12},{16,18},{18,... | collective-permute-start | bytes 1572872 | tf_op jit(solution)/shard_map/ppermute | solution.py:22
  73.0 20.8 %collective-permute-start.14 = (bf16[1024,256]{1,0:T(8,128)(2,1)}, bf16[1024,256]{1,0:T(8,128)(2,1)}, u32[]{:S(2)}, u32[]{:S(2)}) collective-permute-start(bf16[1024,256]{1,0:T(8,128)(2,1)} %fusion.6.y_ref), channel_id=1, source_target_pairs={{0,4},{2,6},{4,0},{6,2},{8,12},{10,14},{12,8},{14,10},{16,20},{18,... | collective-permute-start | bytes 1572872 | tf_op jit(solution)/shard_map/ppermute | solution.py:22
  82.1 18.8 %collective-permute-start.16 = (bf16[1024,256]{1,0:T(8,128)(2,1)S(1)}, bf16[1024,256]{1,0:T(8,128)(2,1)S(1)}, u32[]{:S(2)}, u32[]{:S(2)}) collective-permute-start(bf16[1024,256]{1,0:T(8,128)(2,1)S(1)} %fusion.11), channel_id=1, source_target_pairs={{0,4},{2,6},{4,0},{6,2},{8,12},{10,14},{12,8},{14,10},{16,20},{18,... | collective-permute-start | bytes 1572872 | tf_op jit(solution)/shard_map/ppermute | solution.py:22
  84.3 16.8 %collective-permute-start.17 = (bf16[1024,256]{1,0:T(8,128)(2,1)S(1)}, bf16[1024,256]{1,0:T(8,128)(2,1)S(1)}, u32[]{:S(2)}, u32[]{:S(2)}) collective-permute-start(bf16[1024,256]{1,0:T(8,128)(2,1)S(1)} %fusion.16), channel_id=1, source_target_pairs={{0,2},{2,0},{4,6},{6,4},{8,10},{10,8},{12,14},{14,12},{16,18},{18,... | collective-permute-start | bytes 1572872 | tf_op jit(solution)/shard_map/ppermute | solution.py:22
  90.9 10.6 %collective-permute-start.13 = (bf16[128,2560]{1,0:T(8,128)(2,1)S(1)}, bf16[128,2560]{1,0:T(8,128)(2,1)S(1)}, u32[]{:S(2)}, u32[]{:S(2)}) collective-permute-start(bf16[128,2560]{1,0:T(8,128)(2,1)S(1)} %select_convert_fusion), channel_id=1, source_target_pairs={{0,1},{1,0},{2,3},{3,2},{4,5},{5,4},{6,7},{7,6},{8,9},{9,8},{10,11... | collective-permute-start | bytes 1966088 | tf_op jit(solution)/shard_map/ppermute | solution.py:22
  (19 other events, 94.5 us)
